TPU v7x, 32 devices: a whole 2x2x4 slice. The times are simulated.
32 devices in a mesh: dp: 16 (over z, x, core), mp: 2 (over y).
Axes of the slice: x: 2, y: 2, z: 4, core: 2. Of those that a mesh axis runs over, the one named last changes fastest.
Arguments:
- tokens: bfloat16 [49152, 640], P('dp'), may hold values from -6 to 6
- lengths: int32 [16, 6], P('dp'), may hold values from 0 to 1024, as said below
- gain_one: bfloat16 [640], replicated, may hold values from 0.5 to 1.5
- shift_one: bfloat16 [640], replicated, may hold values from -1 to 1
- w_qkv: bfloat16 [3, 640, 640], P(None, None, 'mp'), may hold values from -0.3125 to 0.3125
- b_qkv: bfloat16 [3, 640], P(None, 'mp'), may hold values from -1.5 to 1.5
- w_out: bfloat16 [640, 640], P('mp'), may hold values from -1 to 1
- b_out: bfloat16 [640], replicated, may hold values from -1 to 1
- gain_two: bfloat16 [640], replicated, may hold values from 0.5 to 1.5
- shift_two: bfloat16 [640], replicated, may hold values from -1 to 1
- w_up: bfloat16 [640, 2560], P(None, 'mp'), may hold values from -0.25 to 0.25
- b_up: bfloat16 [2560], P('mp'), may hold values from -1.5 to 1.5
- w_down: bfloat16 [2560, 640], P('mp'), may hold values from -0.125 to 0.125
- b_down: bfloat16 [640], replicated, may hold values from -1 to 1
- cotangent: bfloat16 [49152, 640], P('dp'), may hold values from -6 to 6
Outputs:
- out_tokens: bfloat16 [49152, 640], P('dp')
- grad_tokens: bfloat16 [49152, 640], P('dp')
- grad_gain_one: float32 [640], replicated
- grad_shift_one: float32 [640], replicated
- grad_w_qkv: float32 [3, 640, 640], P(None, 'dp', 'mp')
- grad_b_qkv: float32 [3, 640], P(None, 'mp')
- grad_w_out: float32 [640, 640], P('mp', 'dp')
- grad_b_out: float32 [640], replicated
- grad_gain_two: float32 [640], replicated
- grad_shift_two: float32 [640], replicated
- grad_w_up: float32 [640, 2560], P('dp', 'mp')
- grad_b_up: float32 [2560], P('mp')
- grad_w_down: float32 [2560, 640], P('mp', 'dp')
- grad_b_down: float32 [640], replicated
Inputs may be any that keep to these rules, and one draw needn't show every extreme that they name: `lengths`: each window's pair of entries is either (1024, 0), one sequence filling the window, or (512, 512), two sequences; exactly half of all windows hold one sequence.
All inputs are finite; a program needn't handle non-finite values.
Results may differ from a plain program's by a relative error of at most 0.017.
Values may be sent and summed in bfloat16 or wider, within the bound.
A program may use at most 320 MiB of HBM per device.

v0:
```python
import jax
import jax.numpy as jnp
from jax import lax
from jax.sharding import PartitionSpec as P

HD = 32
LONG = 1024


epsilon = 1e-05
rotary_base = 10000.0
root_half = 0.7071067811865476
inverse_root_tau = 0.3989422804014327


def normalize(values):
    centred = values - jnp.mean(values, -1, keepdims=True)
    inverse = lax.rsqrt(jnp.mean(centred * centred, -1, keepdims=True) + epsilon)
    return (centred * inverse, inverse)


def normalize_back(normed, inverse, grad_normed):
    mean_grad = jnp.mean(grad_normed, -1, keepdims=True)
    mean_proj = jnp.mean(grad_normed * normed, -1, keepdims=True)
    return inverse * (grad_normed - mean_grad - normed * mean_proj)


def rotate(values, cosines, sines):
    half_width = values.shape[-1] // 2
    first_half = values[..., :half_width]
    second_half = values[..., half_width:]
    return jnp.concatenate(
        [first_half * cosines - second_half * sines, second_half * cosines + first_half * sines], -1
    )


def masked_scores(queries, keys_rot, later_doc):
    scores = jnp.einsum("qhe,khe->hqk", queries, keys_rot, preferred_element_type=jnp.float32)
    same_doc = later_doc[:, None] == later_doc[None, :]
    return jnp.where(same_doc[None], scores, -1e30)


def window_forward(packed):
    queries, keys_rot, values, later_doc = packed
    scores = masked_scores(queries, keys_rot, later_doc)
    row_max = jnp.max(scores, -1, keepdims=True)
    expo_vals = jnp.exp(scores - row_max)
    row_total = jnp.sum(expo_vals, -1, keepdims=True)
    probs = (expo_vals / row_total).astype(jnp.bfloat16)
    out_vals = jnp.einsum("hqk,khe->qhe", probs, values, preferred_element_type=jnp.float32)
    return (out_vals.astype(jnp.bfloat16), (row_max + jnp.log(row_total))[..., 0])


def window_backward(packed):
    queries, keys_rot, values, later_doc, grad_out, log_total = packed
    probs = jnp.exp(masked_scores(queries, keys_rot, later_doc) - log_total[..., None])
    grad_probs = jnp.einsum("qhe,khe->hqk", grad_out, values, preferred_element_type=jnp.float32)
    inner = jnp.sum(probs * grad_probs, -1, keepdims=True)
    grad_scores = (probs * (grad_probs - inner)).astype(jnp.bfloat16)
    grad_q = jnp.einsum("hqk,khe->qhe", grad_scores, keys_rot, preferred_element_type=jnp.float32)
    grad_k = jnp.einsum("hqk,qhe->khe", grad_scores, queries, preferred_element_type=jnp.float32)
    grad_v = jnp.einsum(
        "hqk,qhe->khe", probs.astype(jnp.bfloat16), grad_out, preferred_element_type=jnp.float32
    )
    return (grad_q, grad_k, grad_v)


def on_device(
    tokens,
    lengths,
    gain_one,
    shift_one,
    w_qkv,
    b_qkv,
    w_out,
    b_out,
    gain_two,
    shift_two,
    w_up,
    b_up,
    w_down,
    b_down,
    cotangent,
):
    row_count = tokens.shape[0]
    windows = row_count // LONG
    per_shard = w_qkv.shape[2]
    heads_here = per_shard // HD
    scale = HD ** (-0.5)
    starts = lengths[0, 0::2]
    inside = jnp.arange(LONG, dtype=jnp.int32)
    later_doc = (inside[None, :] >= starts[:, None]).astype(jnp.int32)
    place_in = (
        (inside[None, :] - starts[:, None] * later_doc).astype(jnp.float32).reshape(row_count)
    )
    frequency = rotary_base ** (-jnp.arange(HD // 2, dtype=jnp.float32) * 2.0 / HD)
    angles = place_in[:, None] * frequency[None, :]
    cosines = jnp.cos(angles)[:, None, :]
    sines = jnp.sin(angles)[:, None, :]
    residual = tokens.astype(jnp.float32)
    normed_one, inverse_one = normalize(residual)
    hidden_one = (normed_one * gain_one + shift_one).astype(jnp.bfloat16)
    projected = (
        jnp.einsum("td,sdc->tsc", hidden_one, w_qkv, preferred_element_type=jnp.float32)
        + b_qkv[None]
    )
    projected = projected.reshape(row_count, 3, heads_here, HD)
    queries = (rotate(projected[:, 0], cosines, sines) * scale).astype(jnp.bfloat16)
    keys_rot = rotate(projected[:, 1], cosines, sines).astype(jnp.bfloat16)
    values = projected[:, 2].astype(jnp.bfloat16)
    shape_win = (windows, LONG, heads_here, HD)
    queries_w = queries.reshape(shape_win)
    keys_w = keys_rot.reshape(shape_win)
    values_w = values.reshape(shape_win)
    attended, log_total = lax.map(window_forward, (queries_w, keys_w, values_w, later_doc))
    attended = attended.reshape(row_count, per_shard)
    heads_sum = lax.psum(
        jnp.dot(attended, w_out, preferred_element_type=jnp.float32).astype(jnp.bfloat16), "mp"
    ).astype(jnp.float32)
    mixed = heads_sum + b_out + residual
    normed_two, inverse_two = normalize(mixed)
    hidden_two = (normed_two * gain_two + shift_two).astype(jnp.bfloat16)
    pre_act = jnp.dot(hidden_two, w_up, preferred_element_type=jnp.float32) + b_up
    active = jax.nn.gelu(pre_act, approximate=False).astype(jnp.bfloat16)
    ffn_total = lax.psum(
        jnp.dot(active, w_down, preferred_element_type=jnp.float32).astype(jnp.bfloat16), "mp"
    ).astype(jnp.float32)
    out_tokens = (ffn_total + b_down + mixed).astype(jnp.bfloat16)
    grad_top = cotangent.astype(jnp.float32)
    grad_w_down = jnp.einsum("tf,td->fd", active, cotangent, preferred_element_type=jnp.float32)
    grad_b_down = jnp.sum(grad_top, 0)
    grad_active = jnp.einsum("td,fd->tf", cotangent, w_down, preferred_element_type=jnp.float32)
    slope = (
        0.5 * (1.0 + lax.erf(pre_act * root_half))
        + pre_act * jnp.exp(-0.5 * pre_act * pre_act) * inverse_root_tau
    )
    grad_pre = (grad_active * slope).astype(jnp.bfloat16)
    grad_b_up = jnp.sum(grad_pre, 0, dtype=jnp.float32)
    grad_w_up = jnp.einsum("td,tf->df", hidden_two, grad_pre, preferred_element_type=jnp.float32)
    grad_hidden_two = lax.psum(
        jnp.einsum("tf,df->td", grad_pre, w_up, preferred_element_type=jnp.float32).astype(
            jnp.bfloat16
        ),
        "mp",
    ).astype(jnp.float32)
    grad_gain_two = jnp.sum(grad_hidden_two * normed_two, 0)
    grad_shift_two = jnp.sum(grad_hidden_two, 0)
    grad_mid = grad_top + normalize_back(normed_two, inverse_two, grad_hidden_two * gain_two)
    grad_mid_low = grad_mid.astype(jnp.bfloat16)
    grad_w_out = jnp.einsum("tc,td->cd", attended, grad_mid_low, preferred_element_type=jnp.float32)
    grad_b_out = jnp.sum(grad_mid, 0)
    grad_attended = jnp.einsum(
        "td,cd->tc", grad_mid_low, w_out, preferred_element_type=jnp.float32
    ).astype(jnp.bfloat16)
    grad_q, grad_k, grad_v = lax.map(
        window_backward,
        (queries_w, keys_w, values_w, later_doc, grad_attended.reshape(shape_win), log_total),
    )
    shape_rows = (row_count, heads_here, HD)
    grad_q = rotate(grad_q.reshape(shape_rows) * scale, cosines, -sines)
    grad_k = rotate(grad_k.reshape(shape_rows), cosines, -sines)
    grad_v = grad_v.reshape(shape_rows)
    grad_proj = (
        jnp.stack([grad_q, grad_k, grad_v], 1).reshape(row_count, 3, per_shard).astype(jnp.bfloat16)
    )
    grad_b_qkv = jnp.sum(grad_proj, 0, dtype=jnp.float32)
    grad_w_qkv = jnp.einsum(
        "td,tsc->sdc", hidden_one, grad_proj, preferred_element_type=jnp.float32
    )
    grad_hidden_one = lax.psum(
        jnp.einsum("tsc,sdc->td", grad_proj, w_qkv, preferred_element_type=jnp.float32).astype(
            jnp.bfloat16
        ),
        "mp",
    ).astype(jnp.float32)
    grad_gain_one = jnp.sum(grad_hidden_one * normed_one, 0)
    grad_shift_one = jnp.sum(grad_hidden_one, 0)
    grad_tokens = (
        grad_mid + normalize_back(normed_one, inverse_one, grad_hidden_one * gain_one)
    ).astype(jnp.bfloat16)
    grad_w_qkv, grad_w_out, grad_w_up, grad_w_down = (
        lax.psum_scatter(grad_w_qkv, "dp", scatter_dimension=1, tiled=True),
        lax.psum_scatter(grad_w_out, "dp", scatter_dimension=1, tiled=True),
        lax.psum_scatter(grad_w_up, "dp", scatter_dimension=0, tiled=True),
        lax.psum_scatter(grad_w_down, "dp", scatter_dimension=1, tiled=True),
    )
    small_sums = lax.psum(
        (
            grad_gain_one,
            grad_shift_one,
            grad_b_qkv,
            grad_b_out,
            grad_gain_two,
            grad_shift_two,
            grad_b_up,
            grad_b_down,
        ),
        "dp",
    )
    return (
        out_tokens,
        grad_tokens,
        small_sums[0],
        small_sums[1],
        grad_w_qkv,
        small_sums[2],
        grad_w_out,
        small_sums[3],
        small_sums[4],
        small_sums[5],
        grad_w_up,
        small_sums[6],
        grad_w_down,
        small_sums[7],
    )


def solution(mesh):
    in_specs = (
        P("dp", None),
        P("dp", None),
        P(),
        P(),
        P(None, None, "mp"),
        P(None, "mp"),
        P("mp", None),
        P(),
        P(),
        P(),
        P(None, "mp"),
        P("mp"),
        P("mp", None),
        P(),
        P("dp", None),
    )
    out_specs = (
        P("dp", None),
        P("dp", None),
        P(),
        P(),
        P(None, "dp", "mp"),
        P(None, "mp"),
        P("mp", "dp"),
        P(),
        P(),
        P(),
        P("dp", "mp"),
        P("mp"),
        P("mp", "dp"),
        P(),
    )
    return jax.shard_map(
        on_device, mesh=mesh, in_specs=in_specs, out_specs=out_specs, check_vma=False
    )
```

profile of v0, /device:TPU:0, one launch (start us, length us, event | category | flops | bytes accessed | tf_op | source)
XLA Modules:
  0.0 1642.0 jit_solution(3446113238052085554)
XLA Ops:
  73.9 166.8 %while.26 = (s32[]{:T(128)}, bf16[3,1024,10,32]{1,3,2,0:T(8,128)(2,1)}, f32[3,10,1024]{2,1,0:T(8,128)}, bf16[3,1024,10,32]{1,3,2,0:T(8,128)(2,1)}, s32[3,1024]{1...) while((s32[]{:T(128)}, ...), condition=%wide.region_5.6_spmd, body=%wide.region_2.5_spmd.sunk | while | flops 1437915136 | bytes 133011560 | solution.py:115
  74.8 17.8 %select_reduce_fusion.2 = (f32[10,1024]{1,0:T(8,128)S(1)}, f32[10,1024,1024]{1,2,0:T(8,128)}) fusion(pred[1024,1024]{0,1:T(8,128)(4,1)S(1)} %broadcast_compare_fusion.4, bf16[3,1024,10,32]{1,3,2,0:T(8,128)(2,1)} %get-tuple-element.415, s32[]{:T(128)S(6)} %copy.106, bf16[3,1024,10,32]{1,3,2,0:T(8,128)(2,1)} %get-tuple-element.414), kind=kOutput, calls=%fused_computation.2.clone.1 | convolution fusion | flops 692049920 | bytes 44344320 | tf_op jit(solution)/shard_map/while/body/eval_jaxpr/qhe,khe->hqk/dot_general | solution.py:38
  92.6 17.4 %fusion.134 = f32[10,1024]{1,0:T(8,128)S(1)} fusion(f32[10,1024,1024]{1,2,0:T(8,128)} %get-tuple-element.379, f32[10,1024]{1,0:T(8,128)S(1)} %get-tuple-element.380, pred[1024,1024]{0,1:T(8,128)(4,1)S(1)} %broadcast_compare_fusion.4), kind=kLoop, calls=%fused_computation.3.clone.1 | loop fusion | flops 31447040 | bytes 43073536 | tf_op jit(solution)/shard_map/while/body/eval_jaxpr/reduce_sum | solution.py:48
  110.0 18.9 %fusion.135 = bf16[3,1024,10,32]{1,3,2,0:T(8,128)(2,1)} fusion(bf16[3,1024,10,32]{1,3,2,0:T(8,128)(2,1)} %get-tuple-element.402, s32[]{:T(128)S(6)} %copy.106, f32[10,1024,1024]{1,2,0:T(8,128)} %get-tuple-element.379, f32[10,1024]{1,0:T(8,128)S(1)} %fusion.134, f32[10,1024]{1,0:T(8,128)S(1)} %get-tuple-element.380, ...), kind=kOutput, calls=%fused_computation.8.clone.1 | convolution fusion | flops 713359360 | bytes 44385280 | tf_op jit(solution)/shard_map/while/body/eval_jaxpr/hqk,khe->qhe/dot_general | solution.py:50
  130.2 17.8 %select_reduce_fusion.2 = (f32[10,1024]{1,0:T(8,128)S(1)}, f32[10,1024,1024]{1,2,0:T(8,128)}) fusion(pred[1024,1024]{0,1:T(8,128)(4,1)S(1)} %broadcast_compare_fusion.4, bf16[3,1024,10,32]{1,3,2,0:T(8,128)(2,1)} %get-tuple-element.415, s32[]{:T(128)S(6)} %copy.106, bf16[3,1024,10,32]{1,3,2,0:T(8,128)(2,1)} %get-tuple-element.414), kind=kOutput, calls=%fused_computation.2.clone.1 | convolution fusion | flops 692049920 | bytes 44344320 | tf_op jit(solution)/shard_map/while/body/eval_jaxpr/qhe,khe->hqk/dot_general | solution.py:38
  148.0 17.4 %fusion.134 = f32[10,1024]{1,0:T(8,128)S(1)} fusion(f32[10,1024,1024]{1,2,0:T(8,128)} %get-tuple-element.379, f32[10,1024]{1,0:T(8,128)S(1)} %get-tuple-element.380, pred[1024,1024]{0,1:T(8,128)(4,1)S(1)} %broadcast_compare_fusion.4), kind=kLoop, calls=%fused_computation.3.clone.1 | loop fusion | flops 31447040 | bytes 43073536 | tf_op jit(solution)/shard_map/while/body/eval_jaxpr/reduce_sum | solution.py:48
  165.4 18.9 %fusion.135 = bf16[3,1024,10,32]{1,3,2,0:T(8,128)(2,1)} fusion(bf16[3,1024,10,32]{1,3,2,0:T(8,128)(2,1)} %get-tuple-element.402, s32[]{:T(128)S(6)} %copy.106, f32[10,1024,1024]{1,2,0:T(8,128)} %get-tuple-element.379, f32[10,1024]{1,0:T(8,128)S(1)} %fusion.134, f32[10,1024]{1,0:T(8,128)S(1)} %get-tuple-element.380, ...), kind=kOutput, calls=%fused_computation.8.clone.1 | convolution fusion | flops 713359360 | bytes 44385280 | tf_op jit(solution)/shard_map/while/body/eval_jaxpr/hqk,khe->qhe/dot_general | solution.py:50
  185.6 17.8 %select_reduce_fusion.2 = (f32[10,1024]{1,0:T(8,128)S(1)}, f32[10,1024,1024]{1,2,0:T(8,128)}) fusion(pred[1024,1024]{0,1:T(8,128)(4,1)S(1)} %broadcast_compare_fusion.4, bf16[3,1024,10,32]{1,3,2,0:T(8,128)(2,1)} %get-tuple-element.415, s32[]{:T(128)S(6)} %copy.106, bf16[3,1024,10,32]{1,3,2,0:T(8,128)(2,1)} %get-tuple-element.414), kind=kOutput, calls=%fused_computation.2.clone.1 | convolution fusion | flops 692049920 | bytes 44344320 | tf_op jit(solution)/shard_map/while/body/eval_jaxpr/qhe,khe->hqk/dot_general | solution.py:38
  203.3 17.4 %fusion.134 = f32[10,1024]{1,0:T(8,128)S(1)} fusion(f32[10,1024,1024]{1,2,0:T(8,128)} %get-tuple-element.379, f32[10,1024]{1,0:T(8,128)S(1)} %get-tuple-element.380, pred[1024,1024]{0,1:T(8,128)(4,1)S(1)} %broadcast_compare_fusion.4), kind=kLoop, calls=%fused_computation.3.clone.1 | loop fusion | flops 31447040 | bytes 43073536 | tf_op jit(solution)/shard_map/while/body/eval_jaxpr/reduce_sum | solution.py:48
  220.7 18.9 %fusion.135 = bf16[3,1024,10,32]{1,3,2,0:T(8,128)(2,1)} fusion(bf16[3,1024,10,32]{1,3,2,0:T(8,128)(2,1)} %get-tuple-element.402, s32[]{:T(128)S(6)} %copy.106, f32[10,1024,1024]{1,2,0:T(8,128)} %get-tuple-element.379, f32[10,1024]{1,0:T(8,128)S(1)} %fusion.134, f32[10,1024]{1,0:T(8,128)S(1)} %get-tuple-element.380, ...), kind=kOutput, calls=%fused_computation.8.clone.1 | convolution fusion | flops 713359360 | bytes 44385280 | tf_op jit(solution)/shard_map/while/body/eval_jaxpr/hqk,khe->qhe/dot_general | solution.py:50
  250.5 105.6 %all-reduce.9.cloned.1.call-done = bf16[3072,640]{1,0:T(8,128)(2,1)} async-done(((bf16[3072,640]{1,0:T(8,128)(2,1)}), bf16[3072,640]{1,0:T(8,128)(2,1)}) %all-reduce.9.cloned.1.call-update) | async-done | bytes 3932176 | tf_op jit(solution)/shard_map/psum | solution.py:117
  364.7 42.7 %fusion.49 = (bf16[3072,1280]{1,0:T(8,128)(2,1)}, f32[3072,1280]{1,0:T(8,128)}) fusion(f32[1280]{0:T(1024)S(1)} %convert_element_type.139, bf16[640,1280]{1,0:T(8,128)(2,1)S(1)} %copy-done, f32[640]{0:T(1024)S(1)} %convert_element_type.137, f32[640]{0:T(1024)S(1)} %convert_element_type.136, f32[3072]{0:T(1024)S(1)} %add_rsqrt_fusion, ...), kind=kOutput, calls=%fused_computation.60 | convolution fusion | flops 5310382080 | bytes 33133056 | tf_op jit(solution)/shard_map/dot_general | solution.py:123
  407.4 13.7 convert_reduce_fusion
  432.3 103.0 %all-reduce.11.cloned.1.call-done = bf16[3072,640]{1,0:T(8,128)(2,1)} async-done(((bf16[3072,640]{1,0:T(8,128)(2,1)}), bf16[3072,640]{1,0:T(8,128)(2,1)}) %all-reduce.11.cloned.1.call-update) | async-done | bytes 3932176 | tf_op jit(solution)/shard_map/psum | solution.py:140
  535.3 9.1 fusion.84
  569.3 513.6 %while.27 = (s32[]{:T(128)}, f32[3,1024,10,32]{1,0,3,2:T(4,128)}, f32[3,1024,10,32]{1,0,3,2:T(4,128)}, bf16[3,1024,10,32]{1,3,2,0:T(8,128)(2,1)}, bf16[3,1024,10...) while((s32[]{:T(128)}, f32[3,1024,10,32]{1,0,3,2:T(4,128)}, ...), condition=%wide.region_15.16_spmd, body=%wide.region_13.15_spmd.sunk | while | flops 3482310656 | bytes 361716960 | solution.py:155
  571.9 17.7 %fusion.144 = f32[10,1024,1024]{1,2,0:T(8,128)} fusion(bf16[3,1024,10,32]{1,3,2,0:T(8,128)(2,1)} %get-tuple-element.447, s32[]{:T(128)S(6)} %copy.118, bf16[3,1024,10,32]{1,3,2,0:T(8,128)(2,1)} %get-tuple-element.445), kind=kOutput, calls=%fused_computation.37.clone.1 | convolution fusion | flops 671088640 | bytes 43254784 | tf_op jit(solution)/shard_map/while/body/eval_jaxpr/qhe,khe->hqk/dot_general | solution.py:38
  589.6 15.7 fusion.145
  605.3 28.5 %multiply_reduce_fusion.3 = (f32[10,1024]{1,0:T(8,128)S(1)}, f32[10,1024,1024]{1,2,0:T(8,128)}) fusion(f32[10,1024,1024]{1,2,0:T(8,128)} %fusion.144, f32[10,1024]{1,0:T(8,128)S(1)} %dynamic-slice_bitcast_fusion.2, pred[1024,1024]{0,1:T(8,128)(4,1)S(1)} %broadcast_compare_fusion.5, bf16[3,1024,10,32]{1,3,2,0:T(8,128)(2,1)} %get-tuple-element.450, ...), kind=kOutput, calls=%fused_computation.22.clone.1 | convolution fusion | flops 713021440 | bytes 86352896 | tf_op jit(solution)/shard_map/while/body/eval_jaxpr/qhe,khe->hqk/dot_general | solution.py:57
  633.9 33.9 %multiply_convert_fusion.2 = bf16[10,1024,1024]{1,2,0:T(8,128)(2,1)} fusion(f32[10,1024,1024]{1,2,0:T(8,128)} %get-tuple-element.391, f32[10,1024,1024]{1,2,0:T(8,128)} %fusion.144, f32[10,1024]{1,0:T(8,128)S(1)} %get-tuple-element.392, f32[10,1024]{1,0:T(8,128)S(1)} %dynamic-slice_bitcast_fusion.2, pred[1024,1024]{0,1:T(8,128)(4,1)S(1)} %broadcast_compare_fusion.5), kind=kLoop, calls=%fused_computation.21.clone.1 | loop fusion | flops 52428800 | bytes 105988096 | tf_op jit(solution)/shard_map/while/body/eval_jaxpr/convert_element_type | solution.py:59
  667.8 10.6 convolution_bitcast_fusion.6
  678.5 9.1 convolution_bitcast_fusion.5
  691.3 24.7 %dynamic_update_slice.30 = f32[3,1024,10,32]{1,0,3,2:T(4,128)} dynamic-update-slice(f32[3,1024,10,32]{1,0,3,2:T(4,128)} %get-tuple-element.431, f32[1,1024,10,32]{1,0,3,2:T(1,128)} %copy.97, s32[]{:T(128)S(6)} %copy.118, s32[]{:T(128)} %constant.61.clone.1..sunk, s32[]{:T(128)} %constant.61.clone.1..sunk, s32[]{:T(128)} %constant.61.clone.1..sunk) | dynamic-update-slice | bytes 2621444 | tf_op jit(solution)/shard_map/while/body/jit(dynamic_update_index_in_dim)/dynamic_update_slice | solution.py:155
  716.0 24.7 %dynamic_update_slice.29 = f32[3,1024,10,32]{1,0,3,2:T(4,128)} dynamic-update-slice(f32[3,1024,10,32]{1,0,3,2:T(4,128)} %get-tuple-element.430, f32[1,1024,10,32]{1,0,3,2:T(1,128)S(1)} %copy.96, s32[]{:T(128)S(6)} %copy.118, s32[]{:T(128)} %constant.61.clone.1..sunk, s32[]{:T(128)} %constant.61.clone.1..sunk, s32[]{:T(128)} %constant.61.clone.1..sunk) | dynamic-update-slice | bytes 2621444 | tf_op jit(solution)/shard_map/while/body/jit(dynamic_update_index_in_dim)/dynamic_update_slice | solution.py:155
  742.9 17.7 %fusion.144 = f32[10,1024,1024]{1,2,0:T(8,128)} fusion(bf16[3,1024,10,32]{1,3,2,0:T(8,128)(2,1)} %get-tuple-element.447, s32[]{:T(128)S(6)} %copy.118, bf16[3,1024,10,32]{1,3,2,0:T(8,128)(2,1)} %get-tuple-element.445), kind=kOutput, calls=%fused_computation.37.clone.1 | convolution fusion | flops 671088640 | bytes 43254784 | tf_op jit(solution)/shard_map/while/body/eval_jaxpr/qhe,khe->hqk/dot_general | solution.py:38
  760.7 15.7 fusion.145
  776.4 28.5 %multiply_reduce_fusion.3 = (f32[10,1024]{1,0:T(8,128)S(1)}, f32[10,1024,1024]{1,2,0:T(8,128)}) fusion(f32[10,1024,1024]{1,2,0:T(8,128)} %fusion.144, f32[10,1024]{1,0:T(8,128)S(1)} %dynamic-slice_bitcast_fusion.2, pred[1024,1024]{0,1:T(8,128)(4,1)S(1)} %broadcast_compare_fusion.5, bf16[3,1024,10,32]{1,3,2,0:T(8,128)(2,1)} %get-tuple-element.450, ...), kind=kOutput, calls=%fused_computation.22.clone.1 | convolution fusion | flops 713021440 | bytes 86352896 | tf_op jit(solution)/shard_map/while/body/eval_jaxpr/qhe,khe->hqk/dot_general | solution.py:57
  804.9 33.9 %multiply_convert_fusion.2 = bf16[10,1024,1024]{1,2,0:T(8,128)(2,1)} fusion(f32[10,1024,1024]{1,2,0:T(8,128)} %get-tuple-element.391, f32[10,1024,1024]{1,2,0:T(8,128)} %fusion.144, f32[10,1024]{1,0:T(8,128)S(1)} %get-tuple-element.392, f32[10,1024]{1,0:T(8,128)S(1)} %dynamic-slice_bitcast_fusion.2, pred[1024,1024]{0,1:T(8,128)(4,1)S(1)} %broadcast_compare_fusion.5), kind=kLoop, calls=%fused_computation.21.clone.1 | loop fusion | flops 52428800 | bytes 105988096 | tf_op jit(solution)/shard_map/while/body/eval_jaxpr/convert_element_type | solution.py:59
  838.9 10.6 convolution_bitcast_fusion.6
  862.3 24.7 %dynamic_update_slice.30 = f32[3,1024,10,32]{1,0,3,2:T(4,128)} dynamic-update-slice(f32[3,1024,10,32]{1,0,3,2:T(4,128)} %get-tuple-element.431, f32[1,1024,10,32]{1,0,3,2:T(1,128)} %copy.97, s32[]{:T(128)S(6)} %copy.118, s32[]{:T(128)} %constant.61.clone.1..sunk, s32[]{:T(128)} %constant.61.clone.1..sunk, s32[]{:T(128)} %constant.61.clone.1..sunk) | dynamic-update-slice | bytes 2621444 | tf_op jit(solution)/shard_map/while/body/jit(dynamic_update_index_in_dim)/dynamic_update_slice | solution.py:155
  887.1 24.7 %dynamic_update_slice.29 = f32[3,1024,10,32]{1,0,3,2:T(4,128)} dynamic-update-slice(f32[3,1024,10,32]{1,0,3,2:T(4,128)} %get-tuple-element.430, f32[1,1024,10,32]{1,0,3,2:T(1,128)S(1)} %copy.96, s32[]{:T(128)S(6)} %copy.118, s32[]{:T(128)} %constant.61.clone.1..sunk, s32[]{:T(128)} %constant.61.clone.1..sunk, s32[]{:T(128)} %constant.61.clone.1..sunk) | dynamic-update-slice | bytes 2621444 | tf_op jit(solution)/shard_map/while/body/jit(dynamic_update_index_in_dim)/dynamic_update_slice | solution.py:155
  914.0 17.7 %fusion.144 = f32[10,1024,1024]{1,2,0:T(8,128)} fusion(bf16[3,1024,10,32]{1,3,2,0:T(8,128)(2,1)} %get-tuple-element.447, s32[]{:T(128)S(6)} %copy.118, bf16[3,1024,10,32]{1,3,2,0:T(8,128)(2,1)} %get-tuple-element.445), kind=kOutput, calls=%fused_computation.37.clone.1 | convolution fusion | flops 671088640 | bytes 43254784 | tf_op jit(solution)/shard_map/while/body/eval_jaxpr/qhe,khe->hqk/dot_general | solution.py:38
  931.7 15.7 fusion.145
  947.4 28.5 %multiply_reduce_fusion.3 = (f32[10,1024]{1,0:T(8,128)S(1)}, f32[10,1024,1024]{1,2,0:T(8,128)}) fusion(f32[10,1024,1024]{1,2,0:T(8,128)} %fusion.144, f32[10,1024]{1,0:T(8,128)S(1)} %dynamic-slice_bitcast_fusion.2, pred[1024,1024]{0,1:T(8,128)(4,1)S(1)} %broadcast_compare_fusion.5, bf16[3,1024,10,32]{1,3,2,0:T(8,128)(2,1)} %get-tuple-element.450, ...), kind=kOutput, calls=%fused_computation.22.clone.1 | convolution fusion | flops 713021440 | bytes 86352896 | tf_op jit(solution)/shard_map/while/body/eval_jaxpr/qhe,khe->hqk/dot_general | solution.py:57
  975.9 33.9 %multiply_convert_fusion.2 = bf16[10,1024,1024]{1,2,0:T(8,128)(2,1)} fusion(f32[10,1024,1024]{1,2,0:T(8,128)} %get-tuple-element.391, f32[10,1024,1024]{1,2,0:T(8,128)} %fusion.144, f32[10,1024]{1,0:T(8,128)S(1)} %get-tuple-element.392, f32[10,1024]{1,0:T(8,128)S(1)} %dynamic-slice_bitcast_fusion.2, pred[1024,1024]{0,1:T(8,128)(4,1)S(1)} %broadcast_compare_fusion.5), kind=kLoop, calls=%fused_computation.21.clone.1 | loop fusion | flops 52428800 | bytes 105988096 | tf_op jit(solution)/shard_map/while/body/eval_jaxpr/convert_element_type | solution.py:59
  1009.9 10.6 convolution_bitcast_fusion.6
  1020.5 9.1 convolution_bitcast_fusion.5
  1033.4 24.7 %dynamic_update_slice.30 = f32[3,1024,10,32]{1,0,3,2:T(4,128)} dynamic-update-slice(f32[3,1024,10,32]{1,0,3,2:T(4,128)} %get-tuple-element.431, f32[1,1024,10,32]{1,0,3,2:T(1,128)} %copy.97, s32[]{:T(128)S(6)} %copy.118, s32[]{:T(128)} %constant.61.clone.1..sunk, s32[]{:T(128)} %constant.61.clone.1..sunk, s32[]{:T(128)} %constant.61.clone.1..sunk) | dynamic-update-slice | bytes 2621444 | tf_op jit(solution)/shard_map/while/body/jit(dynamic_update_index_in_dim)/dynamic_update_slice | solution.py:155
  1058.1 24.7 %dynamic_update_slice.29 = f32[3,1024,10,32]{1,0,3,2:T(4,128)} dynamic-update-slice(f32[3,1024,10,32]{1,0,3,2:T(4,128)} %get-tuple-element.430, f32[1,1024,10,32]{1,0,3,2:T(1,128)S(1)} %copy.96, s32[]{:T(128)S(6)} %copy.118, s32[]{:T(128)} %constant.61.clone.1..sunk, s32[]{:T(128)} %constant.61.clone.1..sunk, s32[]{:T(128)} %constant.61.clone.1..sunk) | dynamic-update-slice | bytes 2621444 | tf_op jit(solution)/shard_map/while/body/jit(dynamic_update_index_in_dim)/dynamic_update_slice | solution.py:155
  1134.7 11.2 convolution_convert_fusion.1
  1153.4 13.4 fusion.98
  1167.2 11.4 fusion.101
  1190.9 52.9 %all-reduce.13.cloned.1.call-done = f32[3,640,320]{2,0,1:T(4,128)} async-done(((f32[3,640,320]{2,0,1:T(4,128)}), f32[3,640,320]{2,0,1:T(4,128)}) %all-reduce.13.cloned.1.call-update) | async-done | bytes 2457616
  1245.5 187.4 %all-reduce.15.cloned.1.call-done = (bf16[3072,640]{1,0:T(8,128)(2,1)}, bf16[3072,640]{1,0:T(8,128)(2,1)}) async-done(((bf16[3072,640]{1,0:T(8,128)(2,1)}, bf16[3072,640]{1,0:T(8,128)(2,1)}), (bf16[3072,640]{1,0:T(8,128)(2,1)}, bf16[3072,640]{1,0:T(8,128)(2,1)})) %all-reduce.15.cloned.1.call-update) | async-done | bytes 7864336 | tf_op jit(solution)/shard_map/psum | solution.py:125
  1439.1 62.6 %all-reduce.2 = (f32[640]{0:T(1024)}, f32[640]{0:T(1024)}, f32[3,320]{1,0:T(4,128)}, f32[640]{0:T(1024)}, f32[640]{0:T(1024)}, /*index=5*/f32[640]{0:T(1024)}, f32[1280]{0:T(1024)}, f32[640]{0:T(1024)}) all-reduce(f32[640]{0:T(1024)S(1)} %get-tuple-element.199, ...), channel_id=1, replica_groups=mesh['dp'=16,'mp'=2] {'dp'}, use_global_device_ids=true, to_apply=%region_20.21 | all-reduce | flops 6080 | bytes 48640 | tf_op jit(solution)/shard_map/psum | solution.py:187
  1501.7 13.1 fusion.78
  1514.8 59.8 %reduce-scatter.8.cloned.1.call-done = f32[1280,40]{0,1:T(8,128)} async-done(((f32[1280,640]{0,1:T(8,128)}), f32[1280,40]{0,1:T(8,128)}) %reduce-scatter.8.cloned.1.call-update) | async-done | bytes 204816 | tf_op jit(solution)/shard_map/reduce_scatter | solution.py:185
  1574.6 60.1 %reduce-scatter.10.cloned.1.call-done = f32[320,40]{0,1:T(8,128)} async-done(((f32[320,640]{0,1:T(8,128)}), f32[320,40]{0,1:T(8,128)}) %reduce-scatter.10.cloned.1.call-update) | async-done | bytes 51216
  (248 shorter events, 230.6 us)
Async XLA Ops:
  7.2 357.5 %copy-start = (bf16[640,1280]{1,0:T(8,128)(2,1)S(1)}, bf16[640,1280]{1,0:T(8,128)(2,1)}, u32[]{:S(2)}) copy-start(bf16[640,1280]{1,0:T(8,128)(2,1)} %param.29) | copy-start | bytes 4915204
  7.2 9.2 copy-start.57
  7.2 348.9 %all-reduce.9.cloned.1.call-start = ((), (), s32[]{:S(2)}) async-start(), calls=%async_computation.3 | async-start | bytes 7864320 | tf_op jit(solution)/shard_map/psum | solution.py:117
  7.3 9.1 copy-start.2
  8.1 13.7 copy-start.37
  9.4 12.4 copy-start.47
  12.8 9.0 copy-start.27
  240.7 9.6 copy-start.26
  250.3 285.0 %all-reduce.11.cloned.1.call-start = ((), (), s32[]{:S(2)}) async-start(), calls=%async_computation.4 | async-start | bytes 7864320 | tf_op jit(solution)/shard_map/psum | solution.py:140
  250.4 293.9 %copy-start.31 = (f32[640]{0:T(1024)}, f32[640]{0:T(1024)S(1)}, u32[]{:S(2)}) copy-start(f32[640]{0:T(1024)S(1)} %convert_element_type.135) | copy-start | bytes 7684
  250.5 293.9 %copy-start.39 = (f32[640]{0:T(1024)}, f32[640]{0:T(1024)S(1)}, u32[]{:S(2)}) copy-start(f32[640]{0:T(1024)S(1)} %convert_element_type.136) | copy-start | bytes 7684
  250.5 114.2 %copy-start.49 = (f32[640]{0:T(1024)}, f32[640]{0:T(1024)S(1)}, u32[]{:S(2)}) copy-start(f32[640]{0:T(1024)S(1)} %convert_element_type.137) | copy-start | bytes 7684
  361.7 182.7 %copy-start.29 = (f32[3072]{0:T(1024)}, f32[3072]{0:T(1024)S(1)}, u32[]{:S(2)}) copy-start(f32[3072]{0:T(1024)S(1)} %broadcast_multiply_fusion.5) | copy-start | bytes 36868
  364.7 179.7 %copy-start.35 = (f32[3072]{0:T(1024)}, f32[3072]{0:T(1024)S(1)}, u32[]{:S(2)}) copy-start(f32[3072]{0:T(1024)S(1)} %add_rsqrt_fusion) | copy-start | bytes 36868
  364.7 42.7 %copy-start.17 = (bf16[3072,640]{1,0:T(8,128)(2,1)S(1)}, bf16[3072,640]{1,0:T(8,128)(2,1)}, u32[]{:S(2)}) copy-start(bf16[3072,640]{1,0:T(8,128)(2,1)} %param.33) | copy-start | bytes 11796484
  364.7 42.7 %copy-start.55 = (bf16[1280,640]{1,0:T(8,128)(2,1)S(1)}, bf16[1280,640]{1,0:T(8,128)(2,1)}, u32[]{:S(2)}) copy-start(bf16[1280,640]{1,0:T(8,128)(2,1)} %param.31) | copy-start | bytes 4915204
  432.2 811.6 %all-reduce.13.cloned.1.call-start = ((), (), s32[]{:S(2)}) async-start(), calls=%async_computation.7 | async-start | bytes 7864320
  535.3 9.1 copy-start.4
  535.3 9.1 copy-start.8
  535.3 9.1 copy-start.9
  544.4 11.2 copy-start.25
  571.9 17.7 %copy-start.10 = (bf16[3,1024,10,32]{1,3,2,0:T(8,128)(2,1)S(1)}, bf16[3,1024,10,32]{1,3,2,0:T(8,128)(2,1)}, u32[]{:S(2)}) copy-start(bf16[3,1024,10,32]{1,3,2,0:T(8,128)(2,1)} %get-tuple-element.449) | copy-start | bytes 5898244 | tf_op jit(solution)/shard_map/while
  571.9 17.7 %copy-start.19 = (bf16[3,1024,10,32]{1,3,2,0:T(8,128)(2,1)S(1)}, bf16[3,1024,10,32]{1,3,2,0:T(8,128)(2,1)}, u32[]{:S(2)}) copy-start(bf16[3,1024,10,32]{1,3,2,0:T(8,128)(2,1)} %get-tuple-element.432) | copy-start | bytes 5898244 | tf_op jit(solution)/shard_map/while
  605.3 28.6 %copy-start.20 = (bf16[3,1024,10,32]{1,3,2,0:T(8,128)(2,1)}, bf16[3,1024,10,32]{1,3,2,0:T(8,128)(2,1)S(1)}, u32[]{:S(2)}) copy-start(bf16[3,1024,10,32]{1,3,2,0:T(8,128)(2,1)S(1)} %fusion.145) | copy-start | bytes 5898244 | tf_op jit(solution)/shard_map/while
  742.9 17.7 %copy-start.10 = (bf16[3,1024,10,32]{1,3,2,0:T(8,128)(2,1)S(1)}, bf16[3,1024,10,32]{1,3,2,0:T(8,128)(2,1)}, u32[]{:S(2)}) copy-start(bf16[3,1024,10,32]{1,3,2,0:T(8,128)(2,1)} %get-tuple-element.449) | copy-start | bytes 5898244 | tf_op jit(solution)/shard_map/while
  742.9 17.7 %copy-start.19 = (bf16[3,1024,10,32]{1,3,2,0:T(8,128)(2,1)S(1)}, bf16[3,1024,10,32]{1,3,2,0:T(8,128)(2,1)}, u32[]{:S(2)}) copy-start(bf16[3,1024,10,32]{1,3,2,0:T(8,128)(2,1)} %get-tuple-element.432) | copy-start | bytes 5898244 | tf_op jit(solution)/shard_map/while
  776.4 28.6 %copy-start.20 = (bf16[3,1024,10,32]{1,3,2,0:T(8,128)(2,1)}, bf16[3,1024,10,32]{1,3,2,0:T(8,128)(2,1)S(1)}, u32[]{:S(2)}) copy-start(bf16[3,1024,10,32]{1,3,2,0:T(8,128)(2,1)S(1)} %fusion.145) | copy-start | bytes 5898244 | tf_op jit(solution)/shard_map/while
  914.0 17.7 %copy-start.10 = (bf16[3,1024,10,32]{1,3,2,0:T(8,128)(2,1)S(1)}, bf16[3,1024,10,32]{1,3,2,0:T(8,128)(2,1)}, u32[]{:S(2)}) copy-start(bf16[3,1024,10,32]{1,3,2,0:T(8,128)(2,1)} %get-tuple-element.449) | copy-start | bytes 5898244 | tf_op jit(solution)/shard_map/while
  914.0 17.7 %copy-start.19 = (bf16[3,1024,10,32]{1,3,2,0:T(8,128)(2,1)S(1)}, bf16[3,1024,10,32]{1,3,2,0:T(8,128)(2,1)}, u32[]{:S(2)}) copy-start(bf16[3,1024,10,32]{1,3,2,0:T(8,128)(2,1)} %get-tuple-element.432) | copy-start | bytes 5898244 | tf_op jit(solution)/shard_map/while
  947.4 28.6 %copy-start.20 = (bf16[3,1024,10,32]{1,3,2,0:T(8,128)(2,1)}, bf16[3,1024,10,32]{1,3,2,0:T(8,128)(2,1)S(1)}, u32[]{:S(2)}) copy-start(bf16[3,1024,10,32]{1,3,2,0:T(8,128)(2,1)S(1)} %fusion.145) | copy-start | bytes 5898244 | tf_op jit(solution)/shard_map/while
  1101.8 14.0 copy-start.22
  1101.8 14.0 copy-start.23
  1134.6 298.2 %all-reduce.15.cloned.1.call-start = ((), (), s32[]{:S(2)}) async-start(), calls=%async_computation.9 | async-start | bytes 15728640 | tf_op jit(solution)/shard_map/psum | solution.py:125
  1134.7 11.2 copy-start.12
  1134.7 11.2 copy-start.14
  1134.7 11.2 copy-start.16
  1134.7 11.2 copy-start.58
  1152.7 362.2 %reduce-scatter.6.cloned.1.call-start = ((), (), s32[]{:S(2)}) async-start(), calls=%async_computation.5 | async-start | bytes 3481600 | tf_op jit(solution)/shard_map/reduce_scatter | solution.py:184
  1166.8 11.9 copy-start.54
  1166.9 11.9 copy-start.60
  1166.9 407.8 %reduce-scatter.8.cloned.1.call-start = ((), (), s32[]{:S(2)}) async-start(), calls=%async_computation.6 | async-start | bytes 3481600 | tf_op jit(solution)/shard_map/reduce_scatter | solution.py:185
  1178.6 456.1 %reduce-scatter.10.cloned.1.call-start = ((), (), s32[]{:S(2)}) async-start(), calls=%async_computation.8 | async-start | bytes 1044480
  1190.9 248.2 %copy-start.41 = (f32[640]{0:T(1024)S(1)}, f32[640]{0:T(1024)}, u32[]{:S(2)}) copy-start(f32[640]{0:T(1024)} %get-tuple-element.197) | copy-start | bytes 7684
  1190.9 248.2 %copy-start.42 = (f32[640]{0:T(1024)S(1)}, f32[640]{0:T(1024)}, u32[]{:S(2)}) copy-start(f32[640]{0:T(1024)} %get-tuple-element.203) | copy-start | bytes 7684
  1190.9 248.2 %copy-start.43 = (f32[640]{0:T(1024)S(1)}, f32[640]{0:T(1024)}, u32[]{:S(2)}) copy-start(f32[640]{0:T(1024)} %get-tuple-element.249) | copy-start | bytes 7684
  1190.9 248.2 %copy-start.44 = (f32[640]{0:T(1024)S(1)}, f32[640]{0:T(1024)}, u32[]{:S(2)}) copy-start(f32[640]{0:T(1024)} %get-tuple-element.265) | copy-start | bytes 7684
  1190.9 248.2 %copy-start.45 = (f32[1280]{0:T(1024)S(1)}, f32[1280]{0:T(1024)}, u32[]{:S(2)}) copy-start(f32[1280]{0:T(1024)} %get-tuple-element.277) | copy-start | bytes 15364
  1501.7 133.0 %copy-start.1 = (bf16[640,1280]{1,0:T(8,128)(2,1)S(1)}, bf16[640,1280]{1,0:T(8,128)(2,1)}, u32[]{:S(2)}) copy-start(bf16[640,1280]{1,0:T(8,128)(2,1)} %param.29) | copy-start | bytes 4915204
  (27 other events, 114.1 us)
Sparse Core Ops, SparseCore 0:
  250.5 105.5 all-reduce.8
  432.4 102.8 all-reduce.10
  1134.8 108.9 all-reduce.12
  1246.7 186.0 all-reduce.14
  1437.6 66.9 reduce-scatter.5
  1508.9 65.7 reduce-scatter.7
  1579.3 55.4 reduce-scatter.9
where the time goes:
time: 1660 us; the launch traced here: 1640 us
  waiting for transfers between devices  569 us (34%)
  matrix products  488 us (29%)
  local copies, waits for them, and re-layouts  260 us (16%)
  other arithmetic  244 us (15%)
  blocking collectives  62.6 us (4%)
    psum x1, waiting for transfers between devices, on_device(): lax.psum(jnp.dot(active, w_down, preferred_element_type=jnp.float32).asty...  187 us
    dynamic_update_slice x12, local copies, waits for them, and re-layouts, on_device(): lax.map(window_backward, (queries_w, keys_w, values_w, later_doc, grad_at...  159 us
    unnamed x9, waiting for transfers between devices  113 us
    dot_general x6, matrix products, masked_scores(): jnp.einsum('qhe,khe->hqk', queries, keys_rot, preferred_element_type=jnp....  106 us
    psum x1, waiting for transfers between devices, on_device(): lax.psum(jnp.dot(attended, w_out, preferred_element_type=jnp.float32).ast...  106 us
    psum x1, waiting for transfers between devices, on_device(): lax.psum(jnp.einsum('tf,df->td', grad_pre, w_up, preferred_element_type=j...  103 us
    convert_element_type x3, other arithmetic, window_backward(): grad_scores = (probs * (grad_probs - inner)).astype(jnp.bfloat16)  102 us
    dot_general x3, matrix products, window_backward(): jnp.einsum('qhe,khe->hqk', grad_out, values, preferred_element_type=jnp.f...  85.6 us
  transfers between devices with their start and end apart: 7, of which 6 were waited for; matrix products, arithmetic and copies ran while one was open for 5% of the time, Pallas kernels for 0%

commit v1 on v0

v1 whole, which is shorter than its diff:
```python
import functools

import jax
import jax.numpy as jnp
import numpy as np
from jax import lax
from jax.experimental import pallas as pl
from jax.experimental.pallas import tpu as pltpu
from jax.sharding import PartitionSpec as P

HD = 32
LONG = 1024
BLK = 512
GROUP = 128
epsilon = 1e-05
rotary_base = 10000.0
log2_e = 1.4426950408889634
ln_2 = 0.6931471805599453

f32 = jnp.float32
bf16 = jnp.bfloat16
NT = (((1,), (1,)), ((), ()))
NN = (((1,), (0,)), ((), ()))
TN = (((0,), (0,)), ((), ()))
VMEM_LIMIT = 60 << 20


def dot(a, b, dims=NN):
    return lax.dot_general(a, b, dims, preferred_element_type=f32)


def rope_tables():
    place = np.arange(LONG, dtype=np.float64)[:, None]
    frequency = rotary_base ** (-np.arange(HD // 2, dtype=np.float64) * 2.0 / HD)
    angles = place * frequency[None, :]
    cosines = np.concatenate([np.cos(angles), np.cos(angles)], 1)
    sines = np.concatenate([-np.sin(angles), np.sin(angles)], 1)
    repeat = GROUP // HD
    return (
        np.tile(cosines, (1, repeat)).astype(np.float32),
        np.tile(sines, (1, repeat)).astype(np.float32),
    )


def swap_halves(x):
    lane = lax.broadcasted_iota(jnp.int32, (1, GROUP), 1)
    low = (lane // (HD // 2)) % 2 == 0
    return jnp.where(low, pltpu.roll(x, GROUP - HD // 2, 1), pltpu.roll(x, HD // 2, 1))


def rotate(x, cosines, sines):
    return x * cosines + swap_halves(x) * sines


def rotate_back(x, cosines, sines):
    return x * cosines - swap_halves(x) * sines


def normalize(values):
    centred = values - jnp.mean(values, -1, keepdims=True)
    inverse = lax.rsqrt(jnp.mean(centred * centred, -1, keepdims=True) + epsilon)
    return (centred * inverse, inverse)


def normalize_back(normed, inverse, grad_normed):
    mean_grad = jnp.mean(grad_normed, -1, keepdims=True)
    mean_proj = jnp.mean(grad_normed * normed, -1, keepdims=True)
    return inverse * (grad_normed - mean_grad - normed * mean_proj)


FLAG, BLOCK, TABLE, PLACE = 0, 3, 7, 11


def project_kernel(sc, x_ref, gain, shift, w_ref, b_ref, cos, sin, q_ref, k_ref, v_ref):
    normed, _ = normalize(x_ref[...].astype(f32))
    hidden = (normed * gain[...] + shift[...]).astype(bf16)
    scale = HD ** (-0.5) * log2_e
    width = w_ref.shape[2]
    for s in range(3):
        out = dot(hidden, w_ref[s]) + b_ref[s : s + 1, :]
        if s == 2:
            v_ref[...] = out.astype(bf16)
            continue
        for j in range(width // GROUP):
            cols = slice(j * GROUP, (j + 1) * GROUP)
            part = rotate(out[:, cols], cos[...], sin[...])
            if s == 0:
                q_ref[:, cols] = (part * scale).astype(bf16)
            else:
                k_ref[:, cols] = part.astype(bf16)


def project(sc, tokens, gain, shift, w, b, cos, sin):
    d = tokens.shape[1]
    rows = 4 * BLK
    whole = lambda *shape: pl.BlockSpec(shape, lambda i, s: (0,) * len(shape))
    table = pl.BlockSpec((BLK, GROUP), lambda i, s: (s[TABLE + i], 0))
    out = pl.BlockSpec((BLK, d), lambda i, s: (i, 0))
    return pl.pallas_call(
        project_kernel,
        grid_spec=pltpu.PrefetchScalarGridSpec(
            num_scalar_prefetch=1,
            grid=(4,),
            in_specs=[
                pl.BlockSpec((BLK, d), lambda i, s: (s[BLOCK + i], 0)),
                whole(1, d),
                whole(1, d),
                whole(3, d, d),
                whole(3, d),
                table,
                table,
            ],
            out_specs=[out, out, out],
        ),
        out_shape=[jax.ShapeDtypeStruct((rows, d), bf16)] * 3,
        compiler_params=pltpu.CompilerParams(vmem_limit_bytes=VMEM_LIMIT),
        cost_estimate=pl.CostEstimate(
            flops=2 * rows * d * 3 * d, bytes_accessed=rows * d * 8, transcendentals=0
        ),
        name="project",
    )(sc, tokens, gain, shift, w, b, cos, sin)


def attend_body(q, k_ref, v_ref, o_ref, l_ref, e_ref, store, start, count):
    lane = lax.broadcasted_iota(jnp.int32, (1, GROUP), 1) // HD
    heads = GROUP // HD
    chunks = count // BLK
    values_t = v_ref[pl.ds(start, count), :].T
    ones = jnp.ones((16, count), bf16)
    outs, inverses = [], []

    def score(h, c):
        keys = k_ref[pl.ds(start + c * BLK, BLK), :]
        scores = dot(jnp.where(lane == h, keys, jnp.zeros_like(keys)), q, NT)
        store[h % 2, c * BLK : (c + 1) * BLK, :] = scores
        return jnp.max(scores.reshape(BLK // 8, 8, BLK), axis=0)

    def score_max(h, c, so_far):
        found = score(h, c)
        return found if so_far is None else jnp.maximum(so_far, found)

    top = None
    for c in range(chunks):
        top = score_max(0, c, top)
    row_max = jnp.max(top, axis=0, keepdims=True)
    for h in range(heads):
        top = None
        total = None
        stacked = jnp.concatenate([values_t[HD * h : HD * (h + 1)], ones], 0)
        for c in range(chunks):
            if h + 1 < heads:
                top = score_max(h + 1, c, top)
            rows = slice(c * BLK, (c + 1) * BLK)
            expo = jnp.exp2(store[h % 2, rows, :] - row_max).astype(bf16)
            e_ref[h, pl.ds(start + c * BLK, BLK), :] = expo
            part = dot(stacked[:, rows], expo)
            total = part if total is None else total + part
        inverse = 1.0 / total[HD : HD + 1]
        outs.append(total[:HD] * inverse)
        inverses.append(jnp.broadcast_to(inverse, (HD, BLK)))
        if h + 1 < heads:
            row_max = jnp.max(top, axis=0, keepdims=True)
    o_ref[...] = jnp.concatenate(outs, 0).T.astype(bf16)
    l_ref[...] = jnp.concatenate(inverses, 0).T


def attend_kernel(sc, q_ref, k_ref, v_ref, o_ref, l_ref, e_ref, store):
    b = pl.program_id(1)
    refs = (k_ref, v_ref, o_ref, l_ref, e_ref, store)

    @pl.when(sc[FLAG + b] == 1)
    def _():
        attend_body(q_ref[...], *refs, 0, LONG)

    @pl.when(sc[FLAG + b] == 0)
    def _():
        start = pl.multiple_of(jnp.where(b == 1, BLK, 0), BLK)
        attend_body(q_ref[...], *refs, start, BLK)


def attend(sc, q, k, v):
    d = q.shape[1]
    groups = d // GROUP
    heads = GROUP // HD
    own = 3 * BLK
    qs = pl.BlockSpec((BLK, GROUP), lambda g, b, s: (b, g))
    ks = pl.BlockSpec((LONG, GROUP), lambda g, b, s: (b // 2, g))
    es = pl.BlockSpec((heads, LONG, BLK), lambda g, b, s: (g * 3 + b, 0, 0))
    return pl.pallas_call(
        attend_kernel,
        grid_spec=pltpu.PrefetchScalarGridSpec(
            num_scalar_prefetch=1,
            grid=(groups, 3),
            in_specs=[qs, ks, ks],
            out_specs=[qs, qs, es],
            scratch_shapes=[pltpu.VMEM((2, LONG, BLK), f32)],
        ),
        out_shape=[
            jax.ShapeDtypeStruct((own, d), bf16),
            jax.ShapeDtypeStruct((own, d), f32),
            jax.ShapeDtypeStruct((groups * 3 * heads, LONG, BLK), bf16),
        ],
        compiler_params=pltpu.CompilerParams(vmem_limit_bytes=VMEM_LIMIT),
        cost_estimate=pl.CostEstimate(
            flops=25_000_000_000, bytes_accessed=80_000_000, transcendentals=31_000_000
        ),
        name="attend",
    )(sc, q, k, v)


def attend_back_body(
    q_ref, k_ref, v_ref, do_ref, o_ref, l_ref, e_ref, cos, sin, dq_ref, prod, dk_sum, dv_sum, start, count
):
    lane = lax.broadcasted_iota(jnp.int32, (1, GROUP), 1) // HD
    heads = GROUP // HD
    q = q_ref[...]
    do = (do_ref[...].astype(f32) * l_ref[...]).astype(bf16)
    both = do.astype(f32) * o_ref[...].astype(f32)
    upper = both.astype(bf16)
    lower = (both - upper.astype(f32)).astype(bf16)
    pick = (
        lax.broadcasted_iota(jnp.int32, (8, GROUP), 0)
        == lax.broadcasted_iota(jnp.int32, (8, GROUP), 1) // HD
    )
    pick = pick.astype(f32).astype(bf16)
    delta = dot(pick, upper, NT) + dot(pick, lower, NT)
    keys_t = k_ref[pl.ds(start, count), :].T
    chunks = count // BLK
    tiles = [(h, c) for h in range(heads) for c in range(chunks)]

    def grad_probs(i):
        h, c = tiles[i]
        values = v_ref[pl.ds(start + c * BLK, BLK), :]
        prod[i % 2] = dot(jnp.where(lane == h, values, jnp.zeros_like(values)), do, NT)

    grad_probs(0)
    dq_t = [None] * heads
    for i, (h, c) in enumerate(tiles):
        if i + 1 < len(tiles):
            grad_probs(i + 1)
        rows = pl.ds(start + c * BLK, BLK)
        expo = e_ref[h, rows, :]
        ds = (expo.astype(f32) * (prod[i % 2] - delta[h : h + 1])).astype(bf16)
        dv_sum[rows, :] += dot(expo, jnp.where(lane == h, do, jnp.zeros_like(do)))
        dk_sum[rows, :] += dot(ds, jnp.where(lane == h, q, jnp.zeros_like(q)))
        part = dot(keys_t[HD * h : HD * (h + 1), c * BLK : (c + 1) * BLK], ds)
        dq_t[h] = part if dq_t[h] is None else dq_t[h] + part
    dq = jnp.concatenate(dq_t, 0).T * (HD ** (-0.5))
    dq_ref[...] = rotate_back(dq, cos[...], sin[...]).astype(bf16)


def attend_back_kernel(
    sc, q_ref, k_ref, v_ref, do_ref, o_ref, l_ref, e_ref, cos, sin, cos0, sin0, cos1, sin1,
    dq_ref, dk_ref, dv_ref, prod, dk_sum, dv_sum,
):
    b = pl.program_id(1)
    refs = (q_ref, k_ref, v_ref, do_ref, o_ref, l_ref, e_ref, cos, sin, dq_ref, prod, dk_sum, dv_sum)

    @pl.when(b != 1)
    def _():
        dk_sum[...] = jnp.zeros_like(dk_sum)
        dv_sum[...] = jnp.zeros_like(dv_sum)

    @pl.when(sc[FLAG + b] == 1)
    def _():
        attend_back_body(*refs, 0, LONG)

    @pl.when(sc[FLAG + b] == 0)
    def _():
        start = pl.multiple_of(jnp.where(b == 1, BLK, 0), BLK)
        attend_back_body(*refs, start, BLK)

    @pl.when(b != 0)
    def _():
        for j, (c, s) in enumerate(((cos0, sin0), (cos1, sin1))):
            rows = slice(j * BLK, (j + 1) * BLK)
            dk = dk_sum[rows, :] * ln_2
            dk_ref[rows, :] = rotate_back(dk, c[...], s[...]).astype(bf16)
            dv_ref[rows, :] = dv_sum[rows, :].astype(bf16)


def attend_back(sc, q, k, v, do, o, inverse, expo, cos, sin):
    d = q.shape[1]
    groups = d // GROUP
    heads = GROUP // HD
    own = 3 * BLK
    rows = 4 * BLK
    qs = pl.BlockSpec((BLK, GROUP), lambda g, b, s: (b, g))
    ks = pl.BlockSpec((LONG, GROUP), lambda g, b, s: (b // 2, g))
    es = pl.BlockSpec((heads, LONG, BLK), lambda g, b, s: (g * 3 + b, 0, 0))
    tq = pl.BlockSpec((BLK, GROUP), lambda g, b, s: (s[TABLE + b], 0))
    t0 = pl.BlockSpec((BLK, GROUP), lambda g, b, s: (s[TABLE + 2 * (b // 2)], 0))
    t1 = pl.BlockSpec((BLK, GROUP), lambda g, b, s: (s[TABLE + 2 * (b // 2) + 1], 0))
    return pl.pallas_call(
        attend_back_kernel,
        grid_spec=pltpu.PrefetchScalarGridSpec(
            num_scalar_prefetch=1,
            grid=(groups, 3),
            in_specs=[qs, ks, ks, qs, qs, qs, es, tq, tq, t0, t0, t1, t1],
            out_specs=[qs, ks, ks],
            scratch_shapes=[
                pltpu.VMEM((2, BLK, BLK), f32),
                pltpu.VMEM((LONG, GROUP), f32),
                pltpu.VMEM((LONG, GROUP), f32),
            ],
        ),
        out_shape=[
            jax.ShapeDtypeStruct((own, d), bf16),
            jax.ShapeDtypeStruct((rows, d), bf16),
            jax.ShapeDtypeStruct((rows, d), bf16),
        ],
        compiler_params=pltpu.CompilerParams(vmem_limit_bytes=VMEM_LIMIT),
        cost_estimate=pl.CostEstimate(
            flops=60_000_000_000, bytes_accessed=100_000_000, transcendentals=0
        ),
        name="attend_back",
    )(sc, q, k, v, do, o, inverse, expo, cos, sin, cos, sin, cos, sin)


def gelu_parts(z):
    density = jnp.exp2(z * z * (-0.5 * log2_e)) * 0.3989422804014327
    t = 1.0 / (1.0 + 0.2316419 * jnp.abs(z))
    poly = t * (
        0.319381530
        + t * (-0.356563782 + t * (1.781477937 + t * (-1.821255978 + t * 1.330274429)))
    )
    tail = density * poly
    cdf = jnp.where(z >= 0, 1.0 - tail, tail)
    return z * cdf, cdf + z * density


def middle_kernel(
    sc, x0, x1, x2, y0, y1, y2, o_ref, w_out, b_out, gain, shift, up_own, up_other, b_up, down_own, down_other, b_down,
    out_ref, mid_ref, do_ref, g_up, g_down, g_out, g_bup, g_small,
    r1, h2, h2t, dyt, acc, back,
):
    i = pl.program_id(0)
    last = pl.num_programs(0) - 1
    xs, ys = (x0, x1, x2), (y0, y1, y2)
    blocks = [slice(j * BLK, (j + 1) * BLK) for j in range(3)]

    @pl.when(i == 0)
    def _():
        for j, rows in enumerate(blocks):
            mixed = dot(o_ref[rows, :], w_out[...]) + b_out[...] + xs[j][...].astype(f32)
            r1[rows, :] = mixed
            normed, _ = normalize(mixed)
            hidden = (normed * gain[...] + shift[...]).astype(bf16)
            h2[rows, :] = hidden
            h2t[:, rows] = hidden.T
            dyt[:, rows] = ys[j][...].T
            acc[rows, :] = jnp.zeros_like(mixed)
            back[rows, :] = jnp.zeros_like(mixed)

    first = i <= last // 2
    w_up = jnp.where(first, up_own[...], up_other[...])
    w_down = jnp.where(first, down_own[...], down_other[...])
    actives, grads = [], []
    col_sum = None
    for j, rows in enumerate(blocks):
        pre = dot(h2[rows, :], w_up) + b_up[...]
        active, slope = gelu_parts(pre)
        active = active.astype(bf16)
        actives.append(active)
        acc[rows, :] += dot(active, w_down)
        grad = (dot(ys[j][...], w_down, NT) * slope).astype(bf16)
        grads.append(grad)
        back[rows, :] += dot(grad, w_up, NT)
        s = jnp.sum(grad.astype(f32), 0, keepdims=True)
        col_sum = s if col_sum is None else col_sum + s
    g_bup[...] = col_sum
    g_up[...] = dot(h2t[...], jnp.concatenate(grads, 0)).astype(g_up.dtype)
    g_down[...] = dot(dyt[...], jnp.concatenate(actives, 0)).astype(g_down.dtype)

    @pl.when(i == last)
    def _():
        sums = [None] * 4
        lows = []
        for j, rows in enumerate(blocks):
            mixed = r1[rows, :]
            place = pl.multiple_of(sc[PLACE + j] * BLK, BLK)
            out_ref[pl.ds(place, BLK), :] = (acc[rows, :] + b_down[...] + mixed).astype(bf16)
            normed, inverse = normalize(mixed)
            top = ys[j][...].astype(f32)
            dh = back[rows, :]
            dr = top + normalize_back(normed, inverse, dh * gain[...])
            mid_ref[rows, :] = dr
            low = dr.astype(bf16)
            lows.append(low)
            do_ref[rows, :] = dot(low, w_out[...], NT).astype(bf16)
            for n, term in enumerate((dh * normed, dh, dr, top)):
                s = jnp.sum(term, 0, keepdims=True)
                sums[n] = s if sums[n] is None else sums[n] + s
        g_out[...] = dot(jnp.concatenate(lows, 0).T, o_ref[...]).astype(g_out.dtype)
        g_small[...] = jnp.concatenate(sums + [jnp.zeros_like(sums[0])] * 4, 0)


def middle(sc, tokens, cotangent, o, w_out, b_out, gain, shift, up_own, up_other, b_up, down_own, down_other, b_down):
    d = tokens.shape[1]
    own = 3 * BLK
    half = up_own.shape[1]
    chunk = 256
    per = half // chunk
    one = pl.Buffered(buffer_count=1)
    whole = lambda *shape: pl.BlockSpec(shape, lambda i, s: (0,) * len(shape), pipeline_mode=one)
    rows_of = lambda j: pl.BlockSpec((BLK, d), lambda i, s: (s[BLOCK + j], 0), pipeline_mode=one)
    fixed = lambda *shape: pl.BlockSpec(shape, lambda i, s: (0,) * len(shape))
    low = lambda i: jnp.minimum(i, per - 1)
    high = lambda i: jnp.maximum(i - per, 0)
    return pl.pallas_call(
        middle_kernel,
        grid_spec=pltpu.PrefetchScalarGridSpec(
            num_scalar_prefetch=1,
            grid=(2 * per,),
            in_specs=[rows_of(0), rows_of(1), rows_of(2)] * 2
            + [
                whole(own, d),
                whole(d, d),
                whole(1, d),
                whole(1, d),
                whole(1, d),
                pl.BlockSpec((d, chunk), lambda i, s: (0, low(i))),
                pl.BlockSpec((d, chunk), lambda i, s: (0, high(i))),
                pl.BlockSpec((1, chunk), lambda i, s: (0, i)),
                pl.BlockSpec((chunk, d), lambda i, s: (low(i), 0)),
                pl.BlockSpec((chunk, d), lambda i, s: (high(i), 0)),
                whole(1, d),
            ],
            out_specs=[
                fixed(own, d),
                fixed(own, d),
                fixed(own, d),
                pl.BlockSpec((d, chunk), lambda i, s: (0, i)),
                pl.BlockSpec((d, chunk), lambda i, s: (0, i)),
                fixed(d, d),
                pl.BlockSpec((1, chunk), lambda i, s: (0, i)),
                fixed(8, d),
            ],
            scratch_shapes=[
                pltpu.VMEM((own, d), f32),
                pltpu.VMEM((own, d), bf16),
                pltpu.VMEM((d, own), bf16),
                pltpu.VMEM((d, own), bf16),
                pltpu.VMEM((own, d), f32),
                pltpu.VMEM((own, d), f32),
            ],
        ),
        out_shape=[
            jax.ShapeDtypeStruct((own, d), bf16),
            jax.ShapeDtypeStruct((own, d), f32),
            jax.ShapeDtypeStruct((own, d), bf16),
            jax.ShapeDtypeStruct((d, 2 * half), bf16),
            jax.ShapeDtypeStruct((d, 2 * half), bf16),
            jax.ShapeDtypeStruct((d, d), bf16),
            jax.ShapeDtypeStruct((1, 2 * half), f32),
            jax.ShapeDtypeStruct((8, d), f32),
        ],
        compiler_params=pltpu.CompilerParams(vmem_limit_bytes=VMEM_LIMIT),
        cost_estimate=pl.CostEstimate(
            flops=2 * own * d * (3 * d + 12 * half), bytes_accessed=40_000_000, transcendentals=8_000_000
        ),
        name="middle",
    )(sc, tokens, tokens, tokens, cotangent, cotangent, cotangent, o, w_out, b_out, gain, shift,
      up_own, up_other, b_up, down_own, down_other, b_down)


def project_back_kernel(sc, x_ref, gain, shift, w_ref, dq_ref, dk_ref, dv_ref, dh_ref, g_ref, gb_ref, total, bias):
    i = pl.program_id(0)
    last = pl.num_programs(0) - 1
    d = x_ref.shape[1]
    normed, _ = normalize(x_ref[...].astype(f32))
    hidden_t = (normed * gain[...] + shift[...]).astype(bf16).T

    @pl.when(i == 0)
    def _():
        total[...] = jnp.zeros_like(total)
        bias[...] = jnp.zeros_like(bias)

    def add(s, part):
        cols = slice(s * d, (s + 1) * d)
        total[:, cols] += dot(hidden_t, part)
        bias[:, cols] += jnp.sum(part.astype(f32), 0, keepdims=True)
        return dot(part, w_ref[s], NT)

    dh_ref[...] = add(1, dk_ref[...]) + add(2, dv_ref[...])

    @pl.when(i < last)
    def _():
        dh_ref[...] += add(0, dq_ref[...])

    @pl.when(i == last)
    def _():
        g_ref[...] = total[...].astype(g_ref.dtype)
        gb_ref[...] = bias[...]


def project_back(sc, tokens, gain, shift, w, dq, dk, dv):
    d = tokens.shape[1]
    rows = 4 * BLK
    one = pl.Buffered(buffer_count=1)
    whole = lambda *shape: pl.BlockSpec(shape, lambda i, s: (0,) * len(shape), pipeline_mode=one)
    fixed = lambda *shape: pl.BlockSpec(shape, lambda i, s: (0,) * len(shape))
    block = pl.BlockSpec((BLK, d), lambda i, s: (i, 0))
    return pl.pallas_call(
        project_back_kernel,
        grid_spec=pltpu.PrefetchScalarGridSpec(
            num_scalar_prefetch=1,
            grid=(4,),
            in_specs=[
                pl.BlockSpec((BLK, d), lambda i, s: (s[BLOCK + i], 0)),
                whole(1, d),
                whole(1, d),
                whole(3, d, d),
                pl.BlockSpec((BLK, d), lambda i, s: (jnp.minimum(i, 2), 0)),
                block,
                block,
            ],
            out_specs=[block, fixed(d, 3 * d), fixed(1, 3 * d)],
            scratch_shapes=[pltpu.VMEM((d, 3 * d), f32), pltpu.VMEM((1, 3 * d), f32)],
        ),
        out_shape=[
            jax.ShapeDtypeStruct((rows, d), f32),
            jax.ShapeDtypeStruct((d, 3 * d), bf16),
            jax.ShapeDtypeStruct((1, 3 * d), f32),
        ],
        compiler_params=pltpu.CompilerParams(vmem_limit_bytes=VMEM_LIMIT),
        cost_estimate=pl.CostEstimate(
            flops=4 * rows * d * 3 * d, bytes_accessed=20_000_000, transcendentals=0
        ),
        name="project_back",
    )(sc, tokens, gain, shift, w, dq, dk, dv)


def finish_kernel(sc, x_ref, gain, dh_ref, arrived, mid_ref, out_ref, small):
    i = pl.program_id(0)
    last = pl.num_programs(0) - 1

    @pl.when(i == 0)
    def _():
        small[...] = jnp.zeros_like(small)

    normed, inverse = normalize(x_ref[...].astype(f32))
    dh = dh_ref[...] + jnp.where(i == last, arrived[...].astype(f32), 0.0)
    out_ref[...] = (mid_ref[...] + normalize_back(normed, inverse, dh * gain[...])).astype(bf16)
    small[0:1, :] += jnp.sum(dh * normed, 0, keepdims=True)
    small[1:2, :] += jnp.sum(dh, 0, keepdims=True)


def finish(sc, tokens, gain, dh, arrived, mid):
    d = tokens.shape[1]
    own = 3 * BLK
    block = pl.BlockSpec((BLK, d), lambda i, s: (i, 0))
    return pl.pallas_call(
        finish_kernel,
        grid_spec=pltpu.PrefetchScalarGridSpec(
            num_scalar_prefetch=1,
            grid=(3,),
            in_specs=[
                pl.BlockSpec((BLK, d), lambda i, s: (s[BLOCK + i], 0)),
                pl.BlockSpec((1, d), lambda i, s: (0, 0)),
                block,
                pl.BlockSpec((BLK, d), lambda i, s: (0, 0)),
                block,
            ],
            out_specs=[
                pl.BlockSpec((BLK, d), lambda i, s: (s[PLACE + i], 0)),
                pl.BlockSpec((8, d), lambda i, s: (0, 0)),
            ],
        ),
        out_shape=[jax.ShapeDtypeStruct((own, d), bf16), jax.ShapeDtypeStruct((8, d), f32)],
        compiler_params=pltpu.CompilerParams(vmem_limit_bytes=VMEM_LIMIT),
        cost_estimate=pl.CostEstimate(flops=20_000_000, bytes_accessed=14_000_000, transcendentals=0),
        name="finish",
    )(sc, tokens, gain, dh, arrived, mid)


def on_device(
    tokens, lengths, gain_one, shift_one, w_qkv, b_qkv, w_out, b_out, gain_two, shift_two, w_up, b_up, w_down, b_down,
    cotangent,
):
    d = tokens.shape[1]
    n_dp = lax.axis_size("dp")
    here = lax.axis_index("dp")
    mp = lax.axis_index("mp")
    swap = [(0, 1), (1, 0)]
    half = w_qkv.shape[2]
    hidden = w_up.shape[1]

    long = (lengths[0, 0::2] == LONG).astype(jnp.int32)
    side = jnp.where(mp == 0, long[0], long[2])
    mid = long[1]
    zero = jnp.zeros((), jnp.int32)
    pick = lambda a, b: jnp.where(mp == 0, jnp.array(a, jnp.int32), jnp.array(b, jnp.int32))
    sc = jnp.concatenate(
        [
            jnp.stack([side, side, mid]),
            pick([0, 1, 2, 3], [4, 5, 3, 2]),
            jnp.stack([zero, side, jnp.where(mp == 0, 0, mid), jnp.where(mp == 0, mid, 0)]),
            pick([0, 1, 2], [1, 2, 0]),
        ]
    ).astype(jnp.int32)

    def other(own):
        share = own.shape[0] // n_dp
        piece = lax.dynamic_slice_in_dim(own, here * share, share, 0)
        return lax.all_gather(lax.ppermute(piece, "mp", swap), "dp", tiled=True)

    w_qkv_rows = jnp.transpose(w_qkv, (1, 0, 2)).reshape(d, 3 * half)
    qkv_other = jnp.transpose(other(w_qkv_rows).reshape(d, 3, half), (1, 0, 2))
    w_qkv_all = jnp.concatenate([w_qkv, qkv_other], 2)
    w_out_other = other(w_out.T).T
    w_out_all = jnp.concatenate([w_out, w_out_other], 0)
    up_other = other(w_up)
    down_other = other(w_down)
    b_qkv_all = jnp.concatenate([b_qkv, lax.ppermute(b_qkv, "mp", swap)], 1).astype(f32)
    b_up_all = jnp.concatenate([b_up, lax.ppermute(b_up, "mp", swap)], 0).astype(f32)[None]

    row = lambda v: v.astype(f32)[None]
    cos, sin = (jnp.asarray(t) for t in rope_tables())
    q, k, v = project(sc, tokens, row(gain_one), row(shift_one), w_qkv_all, b_qkv_all, cos, sin)
    o, inverse, expo = attend(sc, q, k, v)
    out_own, grad_mid, do, g_up, g_down, g_out, g_bup, small_two = middle(
        sc, tokens, cotangent, o, w_out_all, row(b_out), row(gain_two), row(shift_two),
        w_up, up_other, b_up_all, w_down, down_other, row(b_down),
    )
    out_tokens = lax.all_gather(out_own, "mp", tiled=True)
    early = lax.psum_scatter(
        jnp.concatenate([g_up, g_down, g_out], 1), "dp", scatter_dimension=0, tiled=True
    )
    dq, dk, dv = attend_back(sc, q, k, v, do, o, inverse, expo, cos, sin)
    dh, g_qkv, g_bqkv = project_back(sc, tokens, row(gain_one), row(shift_one), w_qkv_all, dq, dk, dv)
    arrived = lax.ppermute(dh[3 * BLK :].astype(bf16), "mp", swap)
    grad_own, small_one = finish(sc, tokens, row(gain_one), dh, arrived, grad_mid)
    grad_tokens = lax.all_gather(grad_own, "mp", tiled=True)
    late = lax.psum_scatter(g_qkv, "dp", scatter_dimension=0, tiled=True)

    parts = []
    for block, width in ((early[:, : 2 * hidden], hidden), (early[:, 2 * hidden : 4 * hidden], hidden), (early[:, 4 * hidden :], half)):
        parts.append((block[:, :width], block[:, width:]))
    for s in range(3):
        block = late[:, s * d : (s + 1) * d]
        parts.append((block[:, :half], block[:, half:]))
    mine = jnp.concatenate([a for a, _ in parts], 1)
    theirs = lax.ppermute(jnp.concatenate([b for _, b in parts], 1), "mp", swap)
    total = mine.astype(f32) + theirs.astype(f32)
    grad_w_up = total[:, :hidden]
    grad_w_down = total[:, hidden : 2 * hidden].T
    grad_w_out = total[:, 2 * hidden : 2 * hidden + half].T
    base = 2 * hidden + half
    grad_w_qkv = jnp.stack([total[:, base + s * half : base + (s + 1) * half] for s in range(3)], 0)

    def in_order(v, width):
        v = v.reshape(-1, 2, width)
        return jnp.where(mp == 0, v, v[:, ::-1]).reshape(-1)

    flat = jnp.concatenate(
        [small_one[0], small_one[1], small_two[:4].reshape(-1), in_order(g_bqkv, half), in_order(g_bup, hidden)]
    )
    flat = lax.psum(flat, ("dp", "mp"))
    small = flat[: 6 * d].reshape(6, d)
    g_b = flat[6 * d : 9 * d].reshape(3, 2, half)
    g_u = flat[9 * d :].reshape(2, hidden)
    grad_b_qkv = lax.dynamic_index_in_dim(g_b, mp, 1, keepdims=False)
    grad_b_up = lax.dynamic_index_in_dim(g_u, mp, 0, keepdims=False)
    return (
        out_tokens,
        grad_tokens,
        small[0],
        small[1],
        grad_w_qkv,
        grad_b_qkv,
        grad_w_out,
        small[4],
        small[2],
        small[3],
        grad_w_up,
        grad_b_up,
        grad_w_down,
        small[5],
    )


def solution(mesh):
    in_specs = (
        P("dp", None),
        P("dp", None),
        P(),
        P(),
        P(None, None, "mp"),
        P(None, "mp"),
        P("mp", None),
        P(),
        P(),
        P(),
        P(None, "mp"),
        P("mp"),
        P("mp", None),
        P(),
        P("dp", None),
    )
    out_specs = (
        P("dp", None),
        P("dp", None),
        P(),
        P(),
        P(None, "dp", "mp"),
        P(None, "mp"),
        P("mp", "dp"),
        P(),
        P(),
        P(),
        P("dp", "mp"),
        P("mp"),
        P("mp", "dp"),
        P(),
    )
    return jax.shard_map(on_device, mesh=mesh, in_specs=in_specs, out_specs=out_specs, check_vma=False)
```

time: 1660 us -> 643 us (0.39)
  matrix products: 488 us -> 0 us
  waiting for transfers between devices: 569 us -> 264 us
  other arithmetic: 244 us -> 10.8 us
  local copies, waits for them, and re-layouts: 260 us -> 37.3 us
  Pallas kernels: 0 us -> 193 us
  blocking collectives: 62.6 us -> 99.3 us
    dot_general x33 -> x0, matrix products: 488 us -> none  [the longest x6 106 us: masked_scores(): jnp.einsum('qhe,khe->hqk', queries, keys_rot, preferred_element_type=jnp....]
    psum x3 -> x0, waiting for transfers between devices: 396 us -> none  [the longest x1 187 us: on_device(): lax.psum(jnp.dot(active, w_down, preferred_element_type=jnp.float32).asty...]
    pallas_call x0 -> x6, Pallas kernels: none -> 193 us  [the longest x1 67.1 us: middle(): pl.pallas_call(middle_kernel, grid_spec=pltpu.PrefetchScalarGridSpec(num_...]
    dynamic_update_slice x12 -> x0, local copies, waits for them, and re-layouts: 159 us -> none  [on_device(): lax.map(window_backward, (queries_w, keys_w, values_w, later_doc, grad_at...]
    all_gather x0 -> x5, waiting for transfers between devices: none -> 126 us  [the longest x1 55.2 us: on_device(): grad_tokens = lax.all_gather(grad_own, 'mp', tiled=True)]
    convert_element_type x15 -> x3, other arithmetic: 122 us -> 1.29 us  [the longest x1 0.67 us: on_device(): jnp.concatenate([b_qkv, lax.ppermute(b_qkv, 'mp', swap)], 1).astype(f32)]
    reduce_sum x11 -> x0, other arithmetic: 93.4 us -> none  [the longest x3 52.3 us: window_forward(): row_total = jnp.sum(expo_vals, -1, keepdims=True)]
    reduce_scatter x2 -> x0, waiting for transfers between devices: 59.8 us -> none  [the longest x1 59.8 us: on_device(): lax.psum_scatter(grad_w_down, 'dp', scatter_dimension=1, tiled=True)]
  transfers between devices with their start and end apart: 7 -> 14, of which waited for: 6 -> 7; matrix products, arithmetic and copies ran while one was open for 5% -> 5% of each run, Pallas kernels for 0% -> 8%
where the time goes in v1:
time: 643 us; the launch traced here: 635 us
  waiting for transfers between devices  264 us (41%)
  Pallas kernels  193 us (30%)
  blocking collectives  99.3 us (15%)
  local copies, waits for them, and re-layouts  37.3 us (6%)
  between operations  18.3 us (3%)
  starting transfers between devices  12.3 us (2%)
  other arithmetic  10.8 us (2%)
    unnamed x7, waiting for transfers between devices  121 us
    psum x1, blocking collectives, on_device(): flat = lax.psum(flat, ('dp', 'mp'))  75.6 us
    pallas_call x1, Pallas kernels, middle(): pl.pallas_call(middle_kernel, grid_spec=pltpu.PrefetchScalarGridSpec(num_...  67.1 us
    all_gather x1, waiting for transfers between devices, on_device(): grad_tokens = lax.all_gather(grad_own, 'mp', tiled=True)  55.2 us
    pallas_call x1, Pallas kernels, attend_back(): pl.pallas_call(attend_back_kernel, grid_spec=pltpu.PrefetchScalarGridSpec...  51.3 us
    all_gather x1, waiting for transfers between devices, on_device(): out_tokens = lax.all_gather(out_own, 'mp', tiled=True)  49.4 us
    pallas_call x1, Pallas kernels, attend(): pl.pallas_call(attend_kernel, grid_spec=pltpu.PrefetchScalarGridSpec(num_...  31 us
    all_gather x1, blocking collectives, other(): return lax.all_gather(lax.ppermute(piece, 'mp', swap), 'dp', tiled=True)  23.7 us
  transfers between devices with their start and end apart: 14, of which 7 were waited for; matrix products, arithmetic and copies ran while one was open for 5% of the time, Pallas kernels for 8%

profile of v1, /device:TPU:0, one launch (start us, length us, event | category | flops | bytes accessed | tf_op | source)
XLA Modules:
  0.0 635.4 jit_solution(1830090617690311425)
XLA Ops:
  7.3 1.2 constant_dynamic-slice_fusion.4
  8.5 3.0 collective-permute-start
  11.5 6.0 collective-permute-done
  17.5 0.8 copy.44
  18.3 0.9 constant_dynamic-slice_fusion.2
  19.3 1.7 collective-permute-start.3
  21.0 2.9 collective-permute-done.3
  23.9 0.6 copy-done.5
  24.6 1.8 collective-permute-start.1
  26.7 1.0 constant_dynamic-slice_fusion.3
  27.8 1.8 collective-permute-start.2
  29.6 0.9 constant_dynamic-slice_fusion.1
  30.9 0.7 slice.147
  33.6 0.7 concatenate.42
  34.3 2.5 copy.47
  41.6 1.3 concatenate.38.sc
  42.9 0.7 maximum_convert_fusion.1.b_ref
  44.2 23.7 %all_gather.19 = bf16[640,320]{1,0:T(8,128)(2,1)S(1)} all-gather(bf16[40,320]{1,0:T(8,128)(2,1)S(1)} %collective-permute-done.2), channel_id=1, replica_groups=mesh['dp'=16,'mp'=2] {'dp'}, dimensions={0}, use_global_device_ids=true | all-gather | bytes 435200 | tf_op jit(solution)/shard_map/all_gather | solution.py:606
  68.2 0.6 copy-done.6
  68.9 1.0 pad_maximum_fusion.2.w_out
  69.9 2.4 copy.45
  72.3 2.5 copy.46
  74.8 2.4 pad_maximum_fusion.1.w_ref
  77.2 13.1 %project.1 = (bf16[2048,640]{1,0:T(8,128)(2,1)}, bf16[2048,640]{1,0:T(8,128)(2,1)}, bf16[2048,640]{1,0:T(8,128)(2,1)}) custom-call(s32[14]{0:T(128)} %concatenate.38.sc, bf16[3072,640]{1,0:T(8,128)(2,1)} %x_ref.5, f32[1,640]{1,0:T(1,128)} %reshape.123.gain, f32[1,640]{1,0:T(1,128)} %reshape.124.shift, bf16[3,640,640]{2,1,0:T(8,128)(2,1)} %pad_maximum_fusion.1.w_ref, ...), custom_call_target="tpu_custom_call" | custom-call | flops 5033164800 | bytes 10485760 | tf_op jit(solution)/shard_map/project/pallas_call | solution.py:99
  90.2 31.0 %attend.1 = (bf16[1536,640]{1,0:T(8,128)(2,1)}, f32[1536,640]{1,0:T(8,128)}, bf16[60,1024,512]{2,1,0:T(8,128)(2,1)}) custom-call(s32[14]{0:T(128)} %concatenate.38.sc, bf16[2048,640]{1,0:T(8,128)(2,1)} %get-tuple-element.36.q_ref, bf16[2048,640]{1,0:T(8,128)(2,1)} %get-tuple-element.37.k_ref, bf16[2048,640]{1,0:T(8,128)(2,1)} %get-tuple-element.38.v_ref), custom_call_target="tpu_custom_call" | custom-call | flops 24999999488 | bytes 80000000 | tf_op jit(solution)/shard_map/attend/pallas_call | solution.py:189
  121.2 21.0 %all-gather.10.cloned.1.call-done.down_other = bf16[1280,640]{1,0:T(8,128)(2,1)} async-done(((bf16[80,640]{1,0:T(8,128)(2,1)}), bf16[1280,640]{1,0:T(8,128)(2,1)}) %all-gather.10.cloned.1.call-update) | async-done | bytes 1638416 | tf_op jit(solution)/shard_map/all_gather | solution.py:606
  142.2 67.1 %middle.1 = (bf16[1536,640]{1,0:T(8,128)(2,1)}, f32[1536,640]{1,0:T(8,128)}, bf16[1536,640]{1,0:T(8,128)(2,1)}, bf16[640,2560]{1,0:T(8,128)(2,1)}, bf16[640,2560...) custom-call(s32[14]{0:T(128)} %concatenate.38.sc, bf16[3072,640]{1,0:T(8,128)(2,1)} %x_ref.5, ...), custom_call_target="tpu_custom_call" | custom-call | flops 33973862400 | bytes 40000000 | tf_op jit(solution)/shard_map/middle/pallas_call | solution.py:410
  209.3 51.3 %attend_back.1 = (bf16[1536,640]{1,0:T(8,128)(2,1)}, bf16[2048,640]{1,0:T(8,128)(2,1)}, bf16[2048,640]{1,0:T(8,128)(2,1)}) custom-call(s32[14]{0:T(128)} %concatenate.38.sc, bf16[2048,640]{1,0:T(8,128)(2,1)} %get-tuple-element.36.q_ref, bf16[2048,640]{1,0:T(8,128)(2,1)} %get-tuple-element.37.k_ref, bf16[2048,640]{1,0:T(8,128)(2,1)} %get-tuple-element.38.v_ref, ...), custom_call_target="tpu_custom_call" | custom-call | flops 60000002048 | bytes 100000000 | tf_op jit(solution)/shard_map/attend_back/pallas_call | solution.py:294
  260.6 21.9 %project_back.1 = (f32[2048,640]{1,0:T(8,128)}, bf16[640,1920]{1,0:T(8,128)(2,1)}, f32[1,1920]{1,0:T(1,128)}) custom-call(s32[14]{0:T(128)} %concatenate.38.sc, bf16[3072,640]{1,0:T(8,128)(2,1)} %x_ref.5, f32[1,640]{1,0:T(1,128)} %reshape.123.gain, f32[1,640]{1,0:T(1,128)} %reshape.124.shift, bf16[3,640,640]{2,1,0:T(8,128)(2,1)} %pad_maximum_fusion.1.w_ref, ...), custom_call_target="tpu_custom_call" | custom-call | flops 10066329600 | bytes 20000000 | tf_op jit(solution)/shard_map/project_back/pallas_call | solution.py:504
  282.5 5.4 pad_maximum_fusion
  288.5 1.4 slice.205
  289.9 1.5 collective-permute-start.6
  291.5 9.1 %collective-permute-done.6.arrived = bf16[512,640]{1,0:T(8,128)(2,1)S(1)} collective-permute-done((bf16[512,640]{1,0:T(8,128)(2,1)S(1)}, bf16[512,640]{1,0:T(8,128)(2,1)S(1)}, u32[]{:S(2)}, u32[]{:S(2)}) %collective-permute-start.6) | collective-permute-done | bytes 655392 | tf_op jit(solution)/shard_map/ppermute | solution.py:632
  300.6 0.8 copy-done.3
  301.4 8.9 %finish.1 = (bf16[1536,640]{1,0:T(8,128)(2,1)}, f32[8,640]{1,0:T(8,128)}) custom-call(s32[14]{0:T(128)} %concatenate.38.sc, bf16[3072,640]{1,0:T(8,128)(2,1)} %x_ref.5, f32[1,640]{1,0:T(1,128)} %reshape.123.gain, f32[2048,640]{1,0:T(8,128)} %get-tuple-element.47.dh_ref, bf16[512,640]{1,0:T(8,128)(2,1)} %copy-done.3, f32[1536,640]{1,0:T(8,128)} %get-tuple-element.48.mid_ref), custom_call_target="tpu_custom_call" | custom-call | flops 20000000 | bytes 14000000 | tf_op jit(solution)/shard_map/finish/pallas_call | solution.py:553
  312.3 0.8 slice_reduce_fusion
  313.2 75.6 %psum.7 = f32[8320]{0:T(1024)S(1)} all-reduce(f32[8320]{0:T(1024)S(1)} %constant_dynamic-update-slice_fusion), channel_id=1, replica_groups=mesh['dp'=16,'mp'=2] {'dp','mp'}, use_global_device_ids=true, to_apply=%region_0.1 | all-reduce | flops 8320 | bytes 66560 | tf_op jit(solution)/shard_map/psum | solution.py:659
  389.0 119.9 %all-reduce.5.cloned.1.call-done = (bf16[640,5760]{1,0:T(8,128)(2,1)}, bf16[640,1920]{1,0:T(8,128)(2,1)}) async-done(((bf16[640,5760]{1,0:T(8,128)(2,1)}, bf16[640,1920]{1,0:T(8,128)(2,1)}), (bf16[640,5760]{1,0:T(8,128)(2,1)}, bf16[640,1920]{1,0:T(8,128)(2,1)})) %all-reduce.5.cloned.1.call-update) | async-done | bytes 9830416
  508.9 1.1 fusion
  509.9 1.3 fusion.1
  511.3 1.5 collective-permute-start.7
  514.7 49.4 %all-gather.12.cloned.1.call-done = bf16[3072,640]{1,0:T(8,128)(2,1)} async-done(((bf16[1536,640]{1,0:T(8,128)(2,1)}), bf16[3072,640]{1,0:T(8,128)(2,1)}) %all-gather.12.cloned.1.call-update) | async-done | bytes 3932176 | tf_op jit(solution)/shard_map/all_gather | solution.py:626
  564.1 55.2 %all-gather.14.cloned.1.call-done = bf16[3072,640]{1,0:T(8,128)(2,1)} async-done(((bf16[1536,640]{1,0:T(8,128)(2,1)}), bf16[3072,640]{1,0:T(8,128)(2,1)}) %all-gather.14.cloned.1.call-update) | async-done | bytes 3932176 | tf_op jit(solution)/shard_map/all_gather | solution.py:634
  619.6 0.6 slice_bitcast_fusion.1
  620.2 0.8 slice_bitcast_fusion
  621.0 0.7 pad_maximum_fusion.3
  621.7 4.5 copy.63
  626.2 1.9 copy.64
  (98 shorter events, 10.1 us)
Async XLA Ops:
  7.2 35.8 %copy-start.10 = (bf16[3,320]{1,0:T(4,128)(2,1)S(1)}, bf16[3,320]{1,0:T(4,128)(2,1)}, u32[]{:S(2)}) copy-start(bf16[3,320]{1,0:T(4,128)(2,1)} %param.26) | copy-start | bytes 5764
  7.2 29.6 %copy-start.11 = (bf16[640]{0:T(1024)(128)(2,1)S(1)}, bf16[640]{0:T(1024)(128)(2,1)}, u32[]{:S(2)}) copy-start(bf16[640]{0:T(1024)(128)(2,1)} %param.23) | copy-start | bytes 3844
  7.2 30.2 %copy-start.12 = (bf16[640]{0:T(1024)(128)(2,1)S(1)}, bf16[640]{0:T(1024)(128)(2,1)}, u32[]{:S(2)}) copy-start(bf16[640]{0:T(1024)(128)(2,1)} %param.24) | copy-start | bytes 3844
  7.2 30.8 %copy-start.13 = (bf16[640]{0:T(1024)(128)(2,1)S(1)}, bf16[640]{0:T(1024)(128)(2,1)}, u32[]{:S(2)}) copy-start(bf16[640]{0:T(1024)(128)(2,1)} %param.28) | copy-start | bytes 3844
  7.2 31.3 %copy-start.14 = (bf16[640]{0:T(1024)(128)(2,1)S(1)}, bf16[640]{0:T(1024)(128)(2,1)}, u32[]{:S(2)}) copy-start(bf16[640]{0:T(1024)(128)(2,1)} %param.29) | copy-start | bytes 3844
  7.2 31.9 %copy-start.15 = (bf16[640]{0:T(1024)(128)(2,1)S(1)}, bf16[640]{0:T(1024)(128)(2,1)}, u32[]{:S(2)}) copy-start(bf16[640]{0:T(1024)(128)(2,1)} %param.30) | copy-start | bytes 3844
  7.2 32.5 %copy-start.16 = (bf16[640]{0:T(1024)(128)(2,1)S(1)}, bf16[640]{0:T(1024)(128)(2,1)}, u32[]{:S(2)}) copy-start(bf16[640]{0:T(1024)(128)(2,1)} %param.34) | copy-start | bytes 3844
  7.3 62.6 %all-gather.6.cloned.1.call-start = ((), (), s32[]{:S(2)}) async-start(), calls=%async_computation | async-start | bytes 1392640 | tf_op jit(solution)/shard_map/all_gather | solution.py:606
  8.5 9.0 %collective-permute-start = (bf16[40,960]{0,1:T(8,128)(2,1)S(1)}, bf16[40,960]{0,1:T(8,128)(2,1)S(1)}, u32[]{:S(2)}, u32[]{:S(2)}) collective-permute-start(bf16[40,960]{0,1:T(8,128)(2,1)S(1)} %constant_dynamic-slice_fusion.4), channel_id=1, source_target_pairs={{0,1},{1,0},{2,3},{3,2},{4,5},{5,4},{6,7},{7,6},{8,9},{9,8},{10,11... | collective-permute-start | bytes 230408 | tf_op jit(solution)/shard_map/ppermute | solution.py:606
  18.2 50.6 %copy-start.4 = (bf16[320,640]{1,0:T(8,128)(2,1)S(1)}, bf16[320,640]{1,0:T(8,128)(2,1)}, u32[]{:S(2)}) copy-start(bf16[320,640]{1,0:T(8,128)(2,1)} %param.27) | copy-start | bytes 1228804
  18.3 103.0 %all-gather.8.cloned.1.call-start = ((), (), s32[]{:S(2)}) async-start(), calls=%async_computation.1 | async-start | bytes 1740800 | tf_op jit(solution)/shard_map/all_gather | solution.py:606
  19.3 4.7 collective-permute-start.3
  23.9 0.6 copy-start.5
  24.6 117.6 %all-gather.10.cloned.1.call-start = ((), (), s32[]{:S(2)}) async-start(), calls=%async_computation.2 | async-start | bytes 1740800 | tf_op jit(solution)/shard_map/all_gather | solution.py:606
  24.6 18.3 %collective-permute-start.1 = (bf16[3,320]{1,0:T(4,128)(2,1)}, bf16[3,320]{1,0:T(4,128)(2,1)S(1)}, u32[]{:S(2)}, u32[]{:S(2)}) collective-permute-start(bf16[3,320]{1,0:T(4,128)(2,1)} %param.26), channel_id=1, source_target_pairs={{0,1},{1,0},{2,3},{3,2},{4,5},{5,4},{6,7},{7,6},{8,9},{9,8},{10,11... | collective-permute-start | bytes 5768 | tf_op jit(solution)/shard_map/ppermute | solution.py:615
  26.4 17.2 %collective-permute-start.4 = (bf16[1280]{0:T(1024)(128)(2,1)}, bf16[1280]{0:T(1024)(128)(2,1)S(1)}, u32[]{:S(2)}, u32[]{:S(2)}) collective-permute-start(bf16[1280]{0:T(1024)(128)(2,1)} %param.32), channel_id=1, source_target_pairs={{0,1},{1,0},{2,3},{3,2},{4,5},{5,4},{6,7},{7,6},{8,9},{9,8},{10,11... | collective-permute-start | bytes 7688 | tf_op jit(solution)/shard_map/ppermute | solution.py:616
  27.8 16.4 %collective-permute-start.2 = (bf16[40,320]{1,0:T(8,128)(2,1)S(1)}, bf16[40,320]{1,0:T(8,128)(2,1)S(1)}, u32[]{:S(2)}, u32[]{:S(2)}) collective-permute-start(bf16[40,320]{1,0:T(8,128)(2,1)S(1)} %bitcast.32), channel_id=1, source_target_pairs={{0,1},{1,0},{2,3},{3,2},{4,5},{5,4},{6,7},{7,6},{8,9},{9,8},{10,11... | collective-permute-start | bytes 76808 | tf_op jit(solution)/shard_map/ppermute | solution.py:606
  30.5 37.6 %collective-permute-start.5 = (bf16[80,640]{1,0:T(8,128)(2,1)S(1)}, bf16[80,640]{1,0:T(8,128)(2,1)S(1)}, u32[]{:S(2)}, u32[]{:S(2)}) collective-permute-start(bf16[80,640]{1,0:T(8,128)(2,1)S(1)} %constant_dynamic-slice_fusion.1), channel_id=1, source_target_pairs={{0,1},{1,0},{2,3},{3,2},{4,5},{5,4},{6,7},{7,6},{8,9},{9,8},{10,11... | collective-permute-start | bytes 307208 | tf_op jit(solution)/shard_map/ppermute | solution.py:606
  68.1 0.6 copy-start.6
  68.8 440.0 %all-reduce.5.cloned.1.call-start = ((), (), s32[]{:S(2)}) async-start(), calls=%async_computation.5 | async-start | bytes 19660800
  260.5 21.9 %copy-start.1 = (bf16[640,2560]{1,0:T(8,128)(2,1)S(1)}, bf16[640,2560]{1,0:T(8,128)(2,1)}, u32[]{:S(2)}) copy-start(bf16[640,2560]{1,0:T(8,128)(2,1)} %get-tuple-element.54) | copy-start | bytes 9830404
  260.5 21.9 %copy-start.2 = (bf16[640,640]{1,0:T(8,128)(2,1)S(1)}, bf16[640,640]{1,0:T(8,128)(2,1)}, u32[]{:S(2)}) copy-start(bf16[640,640]{1,0:T(8,128)(2,1)} %get-tuple-element.56) | copy-start | bytes 2457604
  287.9 276.3 %all-gather.12.cloned.1.call-start = ((), (), s32[]{:S(2)}) async-start(), calls=%async_computation.3 | async-start | bytes 5898240 | tf_op jit(solution)/shard_map/all_gather | solution.py:626
  288.5 330.9 %all-gather.14.cloned.1.call-start = ((), (), s32[]{:S(2)}) async-start(), calls=%async_computation.4 | async-start | bytes 5898240 | tf_op jit(solution)/shard_map/all_gather | solution.py:634
  289.9 10.7 %collective-permute-start.6 = (bf16[512,640]{1,0:T(8,128)(2,1)S(1)}, bf16[512,640]{1,0:T(8,128)(2,1)S(1)}, u32[]{:S(2)}, u32[]{:S(2)}) collective-permute-start(bf16[512,640]{1,0:T(8,128)(2,1)S(1)} %slice.205), channel_id=1, source_target_pairs={{0,1},{1,0},{2,3},{3,2},{4,5},{5,4},{6,7},{7,6},{8,9},{9,8},{10,11... | collective-permute-start | bytes 1966088 | tf_op jit(solution)/shard_map/ppermute | solution.py:632
  300.6 0.8 copy-start.3
  301.4 9.0 %copy-start.17 = (u32[32]{0:T(128)S(1)}, u32[32]{0:T(128)}, u32[]{:S(2)}) copy-start(u32[32]{0:T(128)} %constant.50) | copy-start | bytes 388
  301.4 10.2 %copy-start.8 = (f32[1,1920]{1,0:T(1,128)S(1)}, f32[1,1920]{1,0:T(1,128)}, u32[]{:S(2)}) copy-start(f32[1,1920]{1,0:T(1,128)} %get-tuple-element.52) | copy-start | bytes 23044
  301.4 10.3 %copy-start.7 = (f32[1,2560]{1,0:T(1,128)S(1)}, f32[1,2560]{1,0:T(1,128)}, u32[]{:S(2)}) copy-start(f32[1,2560]{1,0:T(1,128)} %get-tuple-element.53) | copy-start | bytes 30724
  301.4 10.9 %copy-start.9 = (f32[8,640]{1,0:T(8,128)S(1)}, f32[8,640]{1,0:T(8,128)}, u32[]{:S(2)}) copy-start(f32[8,640]{1,0:T(8,128)} %get-tuple-element.51) | copy-start | bytes 61444
  511.3 108.2 %collective-permute-start.7 = (bf16[40,3840]{1,0:T(8,128)(2,1)S(1)}, bf16[40,3840]{1,0:T(8,128)(2,1)S(1)}, u32[]{:S(2)}, u32[]{:S(2)}) collective-permute-start(bf16[40,3840]{1,0:T(8,128)(2,1)S(1)} %concatenate.48), channel_id=1, source_target_pairs={{0,1},{1,0},{2,3},{3,2},{4,5},{5,4},{6,7},{7,6},{8,9},{9,8},{10,11... | collective-permute-start | bytes 921608 | tf_op jit(solution)/shard_map/ppermute | solution.py:644
  621.7 4.5 copy-start
Sparse Core Ops, SparseCore 0:
  18.4 41.5 all-gather.5
  62.7 37.7 all-gather.7
  103.2 38.9 all-gather.9
  288.0 220.8 all-reduce.4
  510.3 53.8 all-gather.11
  565.5 53.7 all-gather.13
